TPU v7x, 32 devices: a whole 2x2x4 slice. The times are simulated.
32 devices in a mesh: views: 2 (over x), depth: 2 (over core), lat: 8 (over z, y).
Axes of the slice: x: 2, y: 2, z: 4, core: 2. Of those that a mesh axis runs over, the one named last changes fastest.
Arguments:
- volume: bfloat16 [256, 128, 2048], P(('views', 'depth'), 'lat'), parts along dimension 0, may hold values from -6 to 6
- shift_table: int32 [256], P('views'), parts along dimension 0, may hold values from 0 to 48, as said below
- slab_order: int32 [16, 2], P(('views', 'lat')), parts along dimension 0, may hold values from 0 to 1, each once within a row
- centers: float32 [8], replicated, may hold values from -2 to 2
- widths: float32 [8], replicated, may hold values from 0.5 to 4
- extinct: float32 [8], replicated, may hold values from 0.2 to 3
- colors: float32 [3, 8], replicated, may hold values from 0 to 1
Outputs:
- image: float32 [4, 256, 2048], P(None, ('views', 'lat'), 'depth'), parts along dimension 1
There are 2 independent parts, one for each index of `views`. A program takes and returns all parts, laid end to end along the dimension named above; an argument that names none is the same for every part. Nothing has to cross between parts.
Inputs may be any that keep to these rules, and one draw needn't show every extreme that they name: `shift_table`: every slice's shift lies in 0 to 48; some slice has shift 0 and some slice has shift exactly 48. `slab_order`: each row is a permutation of the slab indices; its entry 0 is the slab nearest the eye for that band of rows.
All inputs are finite; a program needn't handle non-finite values.
Results may differ from a plain program's by a relative error of at most 0.0003.
Values may be sent and summed in bfloat16 or wider, within the bound.
A program may use at most 128 MiB of HBM per device.

v0:
```python
import jax
import jax.numpy as jnp
from jax import lax
from jax.sharding import PartitionSpec as P


def from_behind(block, axis, distance):
    devices = range(lax.axis_size(axis))
    route = [(i - distance, i) for i in devices if i - distance in devices]
    return lax.ppermute(block, axis, route)


def classify(samples, centers, widths, extinct, colors, inv_depth):
    optical = jnp.zeros(samples.shape, jnp.float32)
    emission = jnp.zeros((3,) + samples.shape, jnp.float32)
    for lobe_index in range(centers.shape[0]):
        lobe_value = jnp.exp(-jnp.square(samples - centers[lobe_index]) * widths[lobe_index])
        optical = optical + extinct[lobe_index] * lobe_value
        emission = (
            emission + colors[:, lobe_index].reshape((3,) + (1,) * samples.ndim) * lobe_value[None]
        )
    return (optical * inv_depth, emission)


def take_rows(plane, offset, row_count):
    return lax.dynamic_slice_in_dim(plane, offset, row_count, 0)


def local(volume, shift_table, slab_order, centers, widths, extinct, colors):
    slab_count = lax.axis_size("depth")
    slice_count, row_count, col_count = volume.shape
    slab_start = lax.axis_index("depth") * slice_count
    local_shift = lax.dynamic_slice_in_dim(shift_table, slab_start, slice_count)
    brick_steps = local_shift // row_count
    offsets = local_shift - brick_steps * row_count
    high_bit = (brick_steps // 2 % 2 == 1)[:, None, None]
    low_bit = (brick_steps % 2 == 1)[:, None, None]
    farther = from_behind(volume, "lat", -2)
    held = jnp.where(high_bit, farther, volume)
    nearer = from_behind(held, "lat", -1)
    held = jnp.where(low_bit, nearer, held)
    after = from_behind(held, "lat", -1)
    extended = jnp.concatenate([held, after], axis=1)
    forward = slab_order[0, 0] == 0
    inv_depth = 1.0 / (slice_count * slab_count)
    block_size = 8
    block_count = slice_count // block_size

    def advance(running, counter):
        depth_sum, color = running
        block_index = jnp.where(forward, counter, block_count - 1 - counter)
        block_start = block_index * block_size
        block_cells = lax.dynamic_slice_in_dim(extended, block_start, block_size, 0)
        shifts = lax.dynamic_slice_in_dim(offsets, block_start, block_size)
        samples = jax.vmap(take_rows, in_axes=(0, 0, None))(block_cells, shifts, row_count).astype(
            jnp.float32
        )
        optical, emission = classify(samples, centers, widths, extinct, colors, inv_depth)
        inclusive = jnp.cumsum(optical, axis=0)
        block_total = inclusive[-1]
        before = jnp.where(forward, inclusive - optical, block_total[None] - inclusive)
        weight = jnp.exp(-(depth_sum[None] + before)) * (1.0 - jnp.exp(-optical))
        color = color + jnp.sum(weight[None] * emission, axis=1)
        return ((depth_sum + block_total, color), None)

    start = (
        jnp.zeros((row_count, col_count), jnp.float32),
        jnp.zeros((3, row_count, col_count), jnp.float32),
    )
    (depth_sum, color), _ = lax.scan(advance, start, jnp.arange(block_count, dtype=jnp.int32))
    partial_value = jnp.concatenate([color, depth_sum[None]], axis=0)
    traded = lax.all_to_all(partial_value, "depth", split_axis=2, concat_axis=0, tiled=True)
    front_image = jnp.where(forward, traded[:4], traded[4:])
    back_image = jnp.where(forward, traded[4:], traded[:4])
    rgb_part = front_image[:3] + jnp.exp(-front_image[3])[None] * back_image[:3]
    opacity = 1.0 - jnp.exp(-(front_image[3] + back_image[3]))
    return jnp.concatenate([rgb_part, opacity[None]], axis=0)


def solution(mesh):
    in_specs = (
        P(("views", "depth"), "lat", None),
        P("views"),
        P(("views", "lat"), None),
        P(),
        P(),
        P(),
        P(),
    )
    out_specs = P(None, ("views", "lat"), "depth")
    return jax.shard_map(local, mesh=mesh, in_specs=in_specs, out_specs=out_specs, check_vma=False)
```

profile of v0, /device:TPU:24, one launch (start us, length us, event | category | flops | bytes accessed | tf_op | source)
XLA Modules:
  0.0 849.9 jit_solution(10103599735082312356)
XLA Ops:
  0.0 6.4 copy.76
  6.4 4.3 collective-permute-start
  10.9 88.0 %collective-permute-done = bf16[64,16,2048]{2,0,1:T(8,128)(2,1)} collective-permute-done((bf16[64,16,2048]{2,0,1:T(8,128)(2,1)}, bf16[64,16,2048]{2,0,1:T(8,128)(2,1)}, u32[]{:S(2)}, u32[]{:S(2)}) %collective-permute-start) | collective-permute-done | bytes 4194336 | tf_op jit(solution)/shard_map/ppermute | solution.py:10
  98.9 8.1 broadcast_select_fusion.1
  107.0 5.3 collective-permute-start.1
  112.3 88.9 %collective-permute-done.1 = bf16[64,16,2048]{2,0,1:T(8,128)(2,1)S(1)} collective-permute-done((bf16[64,16,2048]{2,0,1:T(8,128)(2,1)S(1)}, bf16[64,16,2048]{2,0,1:T(8,128)(2,1)S(1)}, u32[]{:S(2)}, u32[]{:S(2)}) %collective-permute-start.1) | collective-permute-done | bytes 4194336 | tf_op jit(solution)/shard_map/ppermute | solution.py:10
  201.3 2.5 broadcast_select_fusion.2
  203.7 5.3 collective-permute-start.2
  209.2 88.1 %collective-permute-done.2 = bf16[64,16,2048]{2,0,1:T(8,128)(2,1)} collective-permute-done((bf16[64,16,2048]{2,0,1:T(8,128)(2,1)}, bf16[64,16,2048]{2,0,1:T(8,128)(2,1)}, u32[]{:S(2)}, u32[]{:S(2)}) %collective-permute-start.2) | collective-permute-done | bytes 4194336 | tf_op jit(solution)/shard_map/ppermute | solution.py:10
  297.4 7.4 pad_maximum_fusion
  304.8 520.3 %while.13 = (s32[]{:T(128)}, f32[16,2048]{1,0:T(8,128)S(1)}, f32[3,16,2048]{2,1,0:T(8,128)S(1)}, f32[8]{0:T(128)S(1)}, s32[8]{0:T(128)S(1)}, /*index=5*/pred[]{:...) while((s32[]{:T(128)}, f32[16,2048]{1,0:T(8,128)S(1)}, ...), condition=%wide.region_3.4_spmd.clone, body=%wide.region_0.3_spmd.clone.sunk | while | flops 51806280 | bytes 49546372 | solution.py:70
  311.7 16.9 %add_multiply_fusion.2 = f32[8,16,2048]{2,0,1:T(8,128)S(1)} fusion(f32[]{:T(128)} %bitcast.108, f32[]{:T(128)} %bitcast.109, f32[]{:T(128)} %bitcast.110, f32[]{:T(128)} %bitcast.111, f32[]{:T(128)} %bitcast.112, f32[]{:T(128)} %bitcast.113, f32[]{:T(128)} %bitcast.114, f32[]{:T(128)} %bitcast.115, f32[]{:T(128)} %bitcast.116, f32[]{:T(128)} %bitcast.117, ...), kind=kLoop, calls=%fused_computation.43.clone.2 | loop fusion | flops 12845056 | bytes 1572960 | tf_op jit(solution)/shard_map/while/body/eval_jaxpr/mul | solution.py:22
  328.6 4.7 reduce_window_sum.13
  333.6 17.4 %subtract_multiply_fusion.2 = f32[8,16,2048]{2,0,1:T(8,128)S(1)} fusion(f32[8,16,2048]{2,0,1:T(8,128)S(1)} %reduce_window_sum.13, f32[16,2048]{1,0:T(8,128)S(1)} %bitcast.137, f32[16,2048]{1,0:T(8,128)S(1)} %get-tuple-element.386, pred[]{:T(512)} %get-tuple-element.426, f32[]{:T(128)} %bitcast.116, f32[]{:T(128)} %bitcast.117, f32[]{:T(128)} %bitcast.108, ...), kind=kLoop, calls=%fused_computation.42.clone.1 | loop fusion | flops 14942208 | bytes 2883681 | tf_op jit(solution)/shard_map/while/body/eval_jaxpr/mul | solution.py:62
  351.6 11.4 %fusion.56 = (f32[8,16,2048]{2,0,1:T(8,128)S(1)}, f32[8,16,2048]{2,0,1:T(8,128)S(1)}, f32[8,16,2048]{2,0,1:T(8,128)S(1)}, f32[8,16,2048]{2,0,1:T(8,128)S(1)}, f3...) fusion(bf16[8,16,2048]{2,0,1:T(8,128)(2,1)S(1)} %gather_fusion,, ...), kind=kLoop, calls=%fused_computation.13.clone.2 | loop fusion | flops 8650752 | bytes 8912960 | tf_op jit(solution)/shard_map/while/body/eval_jaxpr/exp | solution.py:17
  376.7 16.9 %add_multiply_fusion.2 = f32[8,16,2048]{2,0,1:T(8,128)S(1)} fusion(f32[]{:T(128)} %bitcast.108, f32[]{:T(128)} %bitcast.109, f32[]{:T(128)} %bitcast.110, f32[]{:T(128)} %bitcast.111, f32[]{:T(128)} %bitcast.112, f32[]{:T(128)} %bitcast.113, f32[]{:T(128)} %bitcast.114, f32[]{:T(128)} %bitcast.115, f32[]{:T(128)} %bitcast.116, f32[]{:T(128)} %bitcast.117, ...), kind=kLoop, calls=%fused_computation.43.clone.2 | loop fusion | flops 12845056 | bytes 1572960 | tf_op jit(solution)/shard_map/while/body/eval_jaxpr/mul | solution.py:22
  393.6 4.7 reduce_window_sum.13
  398.6 17.4 %subtract_multiply_fusion.2 = f32[8,16,2048]{2,0,1:T(8,128)S(1)} fusion(f32[8,16,2048]{2,0,1:T(8,128)S(1)} %reduce_window_sum.13, f32[16,2048]{1,0:T(8,128)S(1)} %bitcast.137, f32[16,2048]{1,0:T(8,128)S(1)} %get-tuple-element.386, pred[]{:T(512)} %get-tuple-element.426, f32[]{:T(128)} %bitcast.116, f32[]{:T(128)} %bitcast.117, f32[]{:T(128)} %bitcast.108, ...), kind=kLoop, calls=%fused_computation.42.clone.1 | loop fusion | flops 14942208 | bytes 2883681 | tf_op jit(solution)/shard_map/while/body/eval_jaxpr/mul | solution.py:62
  416.6 11.4 %fusion.56 = (f32[8,16,2048]{2,0,1:T(8,128)S(1)}, f32[8,16,2048]{2,0,1:T(8,128)S(1)}, f32[8,16,2048]{2,0,1:T(8,128)S(1)}, f32[8,16,2048]{2,0,1:T(8,128)S(1)}, f3...) fusion(bf16[8,16,2048]{2,0,1:T(8,128)(2,1)S(1)} %gather_fusion,, ...), kind=kLoop, calls=%fused_computation.13.clone.2 | loop fusion | flops 8650752 | bytes 8912960 | tf_op jit(solution)/shard_map/while/body/eval_jaxpr/exp | solution.py:17
  441.7 16.9 %add_multiply_fusion.2 = f32[8,16,2048]{2,0,1:T(8,128)S(1)} fusion(f32[]{:T(128)} %bitcast.108, f32[]{:T(128)} %bitcast.109, f32[]{:T(128)} %bitcast.110, f32[]{:T(128)} %bitcast.111, f32[]{:T(128)} %bitcast.112, f32[]{:T(128)} %bitcast.113, f32[]{:T(128)} %bitcast.114, f32[]{:T(128)} %bitcast.115, f32[]{:T(128)} %bitcast.116, f32[]{:T(128)} %bitcast.117, ...), kind=kLoop, calls=%fused_computation.43.clone.2 | loop fusion | flops 12845056 | bytes 1572960 | tf_op jit(solution)/shard_map/while/body/eval_jaxpr/mul | solution.py:22
  458.6 4.7 reduce_window_sum.13
  463.5 17.4 %subtract_multiply_fusion.2 = f32[8,16,2048]{2,0,1:T(8,128)S(1)} fusion(f32[8,16,2048]{2,0,1:T(8,128)S(1)} %reduce_window_sum.13, f32[16,2048]{1,0:T(8,128)S(1)} %bitcast.137, f32[16,2048]{1,0:T(8,128)S(1)} %get-tuple-element.386, pred[]{:T(512)} %get-tuple-element.426, f32[]{:T(128)} %bitcast.116, f32[]{:T(128)} %bitcast.117, f32[]{:T(128)} %bitcast.108, ...), kind=kLoop, calls=%fused_computation.42.clone.1 | loop fusion | flops 14942208 | bytes 2883681 | tf_op jit(solution)/shard_map/while/body/eval_jaxpr/mul | solution.py:62
  481.5 11.4 %fusion.56 = (f32[8,16,2048]{2,0,1:T(8,128)S(1)}, f32[8,16,2048]{2,0,1:T(8,128)S(1)}, f32[8,16,2048]{2,0,1:T(8,128)S(1)}, f32[8,16,2048]{2,0,1:T(8,128)S(1)}, f3...) fusion(bf16[8,16,2048]{2,0,1:T(8,128)(2,1)S(1)} %gather_fusion,, ...), kind=kLoop, calls=%fused_computation.13.clone.2 | loop fusion | flops 8650752 | bytes 8912960 | tf_op jit(solution)/shard_map/while/body/eval_jaxpr/exp | solution.py:17
  506.7 16.9 %add_multiply_fusion.2 = f32[8,16,2048]{2,0,1:T(8,128)S(1)} fusion(f32[]{:T(128)} %bitcast.108, f32[]{:T(128)} %bitcast.109, f32[]{:T(128)} %bitcast.110, f32[]{:T(128)} %bitcast.111, f32[]{:T(128)} %bitcast.112, f32[]{:T(128)} %bitcast.113, f32[]{:T(128)} %bitcast.114, f32[]{:T(128)} %bitcast.115, f32[]{:T(128)} %bitcast.116, f32[]{:T(128)} %bitcast.117, ...), kind=kLoop, calls=%fused_computation.43.clone.2 | loop fusion | flops 12845056 | bytes 1572960 | tf_op jit(solution)/shard_map/while/body/eval_jaxpr/mul | solution.py:22
  523.6 4.7 reduce_window_sum.13
  528.5 17.4 %subtract_multiply_fusion.2 = f32[8,16,2048]{2,0,1:T(8,128)S(1)} fusion(f32[8,16,2048]{2,0,1:T(8,128)S(1)} %reduce_window_sum.13, f32[16,2048]{1,0:T(8,128)S(1)} %bitcast.137, f32[16,2048]{1,0:T(8,128)S(1)} %get-tuple-element.386, pred[]{:T(512)} %get-tuple-element.426, f32[]{:T(128)} %bitcast.116, f32[]{:T(128)} %bitcast.117, f32[]{:T(128)} %bitcast.108, ...), kind=kLoop, calls=%fused_computation.42.clone.1 | loop fusion | flops 14942208 | bytes 2883681 | tf_op jit(solution)/shard_map/while/body/eval_jaxpr/mul | solution.py:62
  546.5 11.4 %fusion.56 = (f32[8,16,2048]{2,0,1:T(8,128)S(1)}, f32[8,16,2048]{2,0,1:T(8,128)S(1)}, f32[8,16,2048]{2,0,1:T(8,128)S(1)}, f32[8,16,2048]{2,0,1:T(8,128)S(1)}, f3...) fusion(bf16[8,16,2048]{2,0,1:T(8,128)(2,1)S(1)} %gather_fusion,, ...), kind=kLoop, calls=%fused_computation.13.clone.2 | loop fusion | flops 8650752 | bytes 8912960 | tf_op jit(solution)/shard_map/while/body/eval_jaxpr/exp | solution.py:17
  571.6 16.9 %add_multiply_fusion.2 = f32[8,16,2048]{2,0,1:T(8,128)S(1)} fusion(f32[]{:T(128)} %bitcast.108, f32[]{:T(128)} %bitcast.109, f32[]{:T(128)} %bitcast.110, f32[]{:T(128)} %bitcast.111, f32[]{:T(128)} %bitcast.112, f32[]{:T(128)} %bitcast.113, f32[]{:T(128)} %bitcast.114, f32[]{:T(128)} %bitcast.115, f32[]{:T(128)} %bitcast.116, f32[]{:T(128)} %bitcast.117, ...), kind=kLoop, calls=%fused_computation.43.clone.2 | loop fusion | flops 12845056 | bytes 1572960 | tf_op jit(solution)/shard_map/while/body/eval_jaxpr/mul | solution.py:22
  588.6 4.7 reduce_window_sum.13
  593.5 17.4 %subtract_multiply_fusion.2 = f32[8,16,2048]{2,0,1:T(8,128)S(1)} fusion(f32[8,16,2048]{2,0,1:T(8,128)S(1)} %reduce_window_sum.13, f32[16,2048]{1,0:T(8,128)S(1)} %bitcast.137, f32[16,2048]{1,0:T(8,128)S(1)} %get-tuple-element.386, pred[]{:T(512)} %get-tuple-element.426, f32[]{:T(128)} %bitcast.116, f32[]{:T(128)} %bitcast.117, f32[]{:T(128)} %bitcast.108, ...), kind=kLoop, calls=%fused_computation.42.clone.1 | loop fusion | flops 14942208 | bytes 2883681 | tf_op jit(solution)/shard_map/while/body/eval_jaxpr/mul | solution.py:62
  611.5 11.4 %fusion.56 = (f32[8,16,2048]{2,0,1:T(8,128)S(1)}, f32[8,16,2048]{2,0,1:T(8,128)S(1)}, f32[8,16,2048]{2,0,1:T(8,128)S(1)}, f32[8,16,2048]{2,0,1:T(8,128)S(1)}, f3...) fusion(bf16[8,16,2048]{2,0,1:T(8,128)(2,1)S(1)} %gather_fusion,, ...), kind=kLoop, calls=%fused_computation.13.clone.2 | loop fusion | flops 8650752 | bytes 8912960 | tf_op jit(solution)/shard_map/while/body/eval_jaxpr/exp | solution.py:17
  636.6 16.9 %add_multiply_fusion.2 = f32[8,16,2048]{2,0,1:T(8,128)S(1)} fusion(f32[]{:T(128)} %bitcast.108, f32[]{:T(128)} %bitcast.109, f32[]{:T(128)} %bitcast.110, f32[]{:T(128)} %bitcast.111, f32[]{:T(128)} %bitcast.112, f32[]{:T(128)} %bitcast.113, f32[]{:T(128)} %bitcast.114, f32[]{:T(128)} %bitcast.115, f32[]{:T(128)} %bitcast.116, f32[]{:T(128)} %bitcast.117, ...), kind=kLoop, calls=%fused_computation.43.clone.2 | loop fusion | flops 12845056 | bytes 1572960 | tf_op jit(solution)/shard_map/while/body/eval_jaxpr/mul | solution.py:22
  653.6 4.7 reduce_window_sum.13
  658.5 17.4 %subtract_multiply_fusion.2 = f32[8,16,2048]{2,0,1:T(8,128)S(1)} fusion(f32[8,16,2048]{2,0,1:T(8,128)S(1)} %reduce_window_sum.13, f32[16,2048]{1,0:T(8,128)S(1)} %bitcast.137, f32[16,2048]{1,0:T(8,128)S(1)} %get-tuple-element.386, pred[]{:T(512)} %get-tuple-element.426, f32[]{:T(128)} %bitcast.116, f32[]{:T(128)} %bitcast.117, f32[]{:T(128)} %bitcast.108, ...), kind=kLoop, calls=%fused_computation.42.clone.1 | loop fusion | flops 14942208 | bytes 2883681 | tf_op jit(solution)/shard_map/while/body/eval_jaxpr/mul | solution.py:62
  676.5 11.4 %fusion.56 = (f32[8,16,2048]{2,0,1:T(8,128)S(1)}, f32[8,16,2048]{2,0,1:T(8,128)S(1)}, f32[8,16,2048]{2,0,1:T(8,128)S(1)}, f32[8,16,2048]{2,0,1:T(8,128)S(1)}, f3...) fusion(bf16[8,16,2048]{2,0,1:T(8,128)(2,1)S(1)} %gather_fusion,, ...), kind=kLoop, calls=%fused_computation.13.clone.2 | loop fusion | flops 8650752 | bytes 8912960 | tf_op jit(solution)/shard_map/while/body/eval_jaxpr/exp | solution.py:17
  701.6 16.9 %add_multiply_fusion.2 = f32[8,16,2048]{2,0,1:T(8,128)S(1)} fusion(f32[]{:T(128)} %bitcast.108, f32[]{:T(128)} %bitcast.109, f32[]{:T(128)} %bitcast.110, f32[]{:T(128)} %bitcast.111, f32[]{:T(128)} %bitcast.112, f32[]{:T(128)} %bitcast.113, f32[]{:T(128)} %bitcast.114, f32[]{:T(128)} %bitcast.115, f32[]{:T(128)} %bitcast.116, f32[]{:T(128)} %bitcast.117, ...), kind=kLoop, calls=%fused_computation.43.clone.2 | loop fusion | flops 12845056 | bytes 1572960 | tf_op jit(solution)/shard_map/while/body/eval_jaxpr/mul | solution.py:22
  718.5 4.7 reduce_window_sum.13
  723.5 17.4 %subtract_multiply_fusion.2 = f32[8,16,2048]{2,0,1:T(8,128)S(1)} fusion(f32[8,16,2048]{2,0,1:T(8,128)S(1)} %reduce_window_sum.13, f32[16,2048]{1,0:T(8,128)S(1)} %bitcast.137, f32[16,2048]{1,0:T(8,128)S(1)} %get-tuple-element.386, pred[]{:T(512)} %get-tuple-element.426, f32[]{:T(128)} %bitcast.116, f32[]{:T(128)} %bitcast.117, f32[]{:T(128)} %bitcast.108, ...), kind=kLoop, calls=%fused_computation.42.clone.1 | loop fusion | flops 14942208 | bytes 2883681 | tf_op jit(solution)/shard_map/while/body/eval_jaxpr/mul | solution.py:62
  741.5 11.4 %fusion.56 = (f32[8,16,2048]{2,0,1:T(8,128)S(1)}, f32[8,16,2048]{2,0,1:T(8,128)S(1)}, f32[8,16,2048]{2,0,1:T(8,128)S(1)}, f32[8,16,2048]{2,0,1:T(8,128)S(1)}, f3...) fusion(bf16[8,16,2048]{2,0,1:T(8,128)(2,1)S(1)} %gather_fusion,, ...), kind=kLoop, calls=%fused_computation.13.clone.2 | loop fusion | flops 8650752 | bytes 8912960 | tf_op jit(solution)/shard_map/while/body/eval_jaxpr/exp | solution.py:17
  766.6 16.9 %add_multiply_fusion.2 = f32[8,16,2048]{2,0,1:T(8,128)S(1)} fusion(f32[]{:T(128)} %bitcast.108, f32[]{:T(128)} %bitcast.109, f32[]{:T(128)} %bitcast.110, f32[]{:T(128)} %bitcast.111, f32[]{:T(128)} %bitcast.112, f32[]{:T(128)} %bitcast.113, f32[]{:T(128)} %bitcast.114, f32[]{:T(128)} %bitcast.115, f32[]{:T(128)} %bitcast.116, f32[]{:T(128)} %bitcast.117, ...), kind=kLoop, calls=%fused_computation.43.clone.2 | loop fusion | flops 12845056 | bytes 1572960 | tf_op jit(solution)/shard_map/while/body/eval_jaxpr/mul | solution.py:22
  783.5 4.7 reduce_window_sum.13
  788.5 17.4 %subtract_multiply_fusion.2 = f32[8,16,2048]{2,0,1:T(8,128)S(1)} fusion(f32[8,16,2048]{2,0,1:T(8,128)S(1)} %reduce_window_sum.13, f32[16,2048]{1,0:T(8,128)S(1)} %bitcast.137, f32[16,2048]{1,0:T(8,128)S(1)} %get-tuple-element.386, pred[]{:T(512)} %get-tuple-element.426, f32[]{:T(128)} %bitcast.116, f32[]{:T(128)} %bitcast.117, f32[]{:T(128)} %bitcast.108, ...), kind=kLoop, calls=%fused_computation.42.clone.1 | loop fusion | flops 14942208 | bytes 2883681 | tf_op jit(solution)/shard_map/while/body/eval_jaxpr/mul | solution.py:62
  806.4 11.4 %fusion.56 = (f32[8,16,2048]{2,0,1:T(8,128)S(1)}, f32[8,16,2048]{2,0,1:T(8,128)S(1)}, f32[8,16,2048]{2,0,1:T(8,128)S(1)}, f32[8,16,2048]{2,0,1:T(8,128)S(1)}, f3...) fusion(bf16[8,16,2048]{2,0,1:T(8,128)(2,1)S(1)} %gather_fusion,, ...), kind=kLoop, calls=%fused_computation.13.clone.2 | loop fusion | flops 8650752 | bytes 8912960 | tf_op jit(solution)/shard_map/while/body/eval_jaxpr/exp | solution.py:17
  825.1 3.1 copy.79
  828.2 4.8 reshape.133
  833.0 4.2 all_to_all.15
  840.0 5.0 reshape.134
  845.0 3.5 copy.83
  (197 shorter events, 110.6 us)
Async XLA Ops:
  0.0 10.8 %copy-start.4 = (s32[128]{0:T(128)S(1)}, s32[128]{0:T(128)}, u32[]{:S(2)}) copy-start(s32[128]{0:T(128)} %param.10) | copy-start | bytes 1540
  6.4 92.5 %collective-permute-start = (bf16[64,16,2048]{2,0,1:T(8,128)(2,1)}, bf16[64,16,2048]{2,0,1:T(8,128)(2,1)}, u32[]{:S(2)}, u32[]{:S(2)}) collective-permute-start(bf16[64,16,2048]{2,0,1:T(8,128)(2,1)} %copy.76), channel_id=1, source_target_pairs={{2,0},{3,1},{4,2},{5,3},{6,4},{7,5},{10,8},{11,9},{12,10},{13,11},... | collective-permute-start | bytes 12582920 | tf_op jit(solution)/shard_map/ppermute | solution.py:10
  107.0 94.3 %collective-permute-start.1 = (bf16[64,16,2048]{2,0,1:T(8,128)(2,1)S(1)}, bf16[64,16,2048]{2,0,1:T(8,128)(2,1)S(1)}, u32[]{:S(2)}, u32[]{:S(2)}) collective-permute-start(bf16[64,16,2048]{2,0,1:T(8,128)(2,1)S(1)} %broadcast_select_fusion.1), channel_id=1, source_target_pairs={{1,0},{2,1},{3,2},{4,3},{5,4},{6,5},{7,6},{9,8},{10,9},{11,10},{12... | collective-permute-start | bytes 12582920 | tf_op jit(solution)/shard_map/ppermute | solution.py:10
  201.3 7.8 copy-start.3
  201.3 7.9 copy-start.5
  203.7 93.6 %collective-permute-start.2 = (bf16[64,16,2048]{2,0,1:T(8,128)(2,1)}, bf16[64,16,2048]{2,0,1:T(8,128)(2,1)}, u32[]{:S(2)}, u32[]{:S(2)}) collective-permute-start(bf16[64,16,2048]{2,0,1:T(8,128)(2,1)} %broadcast_select_fusion.2), channel_id=1, source_target_pairs={{1,0},{2,1},{3,2},{4,3},{5,4},{6,5},{7,6},{9,8},{10,9},{11,10},{12... | collective-permute-start | bytes 12582920 | tf_op jit(solution)/shard_map/ppermute | solution.py:10
  209.2 95.6 %copy-start = (f32[8]{0:T(128)S(1)}, f32[8]{0:T(128)}, u32[]{:S(2)}) copy-start(f32[8]{0:T(128)} %param.14) | copy-start | bytes 100
  209.2 95.6 %copy-start.1 = (f32[8]{0:T(128)S(1)}, f32[8]{0:T(128)}, u32[]{:S(2)}) copy-start(f32[8]{0:T(128)} %param.12) | copy-start | bytes 100
  209.2 95.6 %copy-start.2 = (f32[8]{0:T(128)S(1)}, f32[8]{0:T(128)}, u32[]{:S(2)}) copy-start(f32[8]{0:T(128)} %param.13) | copy-start | bytes 100
where the time goes:
time: 857 us; the launch traced here: 850 us
  other arithmetic  442 us (52%)
  waiting for transfers between devices  265 us (31%)
  local copies, waits for them, and re-layouts  112 us (13%)
  starting transfers between devices  14.9 us (2%)
  loops' own time  11.7 us (1%)
    ppermute x3, waiting for transfers between devices, from_behind(): return lax.ppermute(block, axis, route)  265 us
    mul x8, other arithmetic, advance(): weight = jnp.exp(-(depth_sum[None] + before)) * (1.0 - jnp.exp(-optical))  139 us
    mul x8, other arithmetic, classify(): return (optical * inv_depth, emission)  135 us
    exp x8, other arithmetic, classify(): jnp.exp(-jnp.square(samples - centers[lobe_index]) * widths[lobe_index])  90.8 us
    exp x64, local copies, waits for them, and re-layouts, classify(): jnp.exp(-jnp.square(samples - centers[lobe_index]) * widths[lobe_index])  39.2 us
    another operation x8, other arithmetic, advance(): inclusive = jnp.cumsum(optical, axis=0)  37.4 us
  transfers between devices with their start and end apart: 3, of which 3 were waited for; matrix products, arithmetic and copies ran while one was open for 0% of the time, Pallas kernels for 0%

commit v1 on v0

v1 whole, which is shorter than its diff:
```python
import jax
import jax.numpy as jnp
from jax import lax
from jax.experimental import pallas as pl
from jax.experimental.pallas import tpu as pltpu
from jax.sharding import PartitionSpec as P

CHUNKS = 4
BLOCK = 256
LANES = 128


def from_behind(block, axis, distance):
    devices = range(lax.axis_size(axis))
    route = [(i - distance, i) for i in devices if i - distance in devices]
    return lax.ppermute(block, axis, route)


def max_over(value, axis):
    size = lax.axis_size(axis)
    best = value
    for step in range(1, size):
        route = [(i, (i + step) % size) for i in range(size)]
        best = jnp.maximum(best, lax.ppermute(value, axis, route))
    return best


def exclusive(counts):
    z = jnp.arange(counts.shape[0], dtype=jnp.int32)
    return jnp.sum(jnp.where(z[None, :] < z[:, None], counts[None, :], 0), axis=1)


def positions(wanted):
    slices, rows = wanted.shape
    ones = wanted.astype(jnp.int32)
    base = exclusive(jnp.sum(ones, axis=1))
    r = jnp.arange(rows, dtype=jnp.int32)
    rank = jnp.sum(jnp.where(r[None, :, None] > r[None, None, :], ones[:, None, :], 0), axis=2)
    return jnp.where(wanted, base[:, None] + rank, -1)


def plan(local_shift, rows):
    source = jnp.arange(rows, dtype=jnp.int32)[None, :]
    target = (source - local_shift[:, None]) % rows
    far = (target + local_shift[:, None]) // rows
    return target, far


def one_hot(place, count):
    return (place.reshape(1, -1) == jnp.arange(count, dtype=jnp.int32)[:, None]).astype(jnp.bfloat16)


def render_kernel(slices, rows, front_ref, par_ref, own_m, two_m, odd_m, own, two, odd, out_ref, cells):
    lobes = par_ref.shape[1]
    tile = 256

    @pl.loop(0, cells.shape[0], step=tile)
    def _(start):
        at = pl.ds(pl.multiple_of(start, tile), tile)
        cells[at, :] = (
            jnp.dot(own_m[at, :], own[...], preferred_element_type=jnp.float32)
            + jnp.dot(two_m[at, :], two[...], preferred_element_type=jnp.float32)
            + jnp.dot(odd_m[at, :], odd[...], preferred_element_type=jnp.float32)
        )

    forward = front_ref[0, 0] == 0
    for part in range(out_ref.shape[2] // LANES):
        lanes = slice(part * LANES, (part + 1) * LANES)

        def advance(i, carry):
            depth, clear, red, green, blue = carry
            z = jnp.where(forward, i, slices - 1 - i)
            samples = cells[pl.ds(pl.multiple_of(z * rows, rows), rows), lanes]
            sums = None
            for k in range(lobes):
                off = samples - par_ref[0, k]
                lobe = jnp.exp(off * off * par_ref[1, k])
                terms = [par_ref[2 + j, k] * lobe for j in range(4)]
                sums = terms if sums is None else [a + b for a, b in zip(sums, terms)]
            depth = depth + sums[0]
            after = jnp.exp(-depth)
            weight = clear - after
            return (depth, after, red + weight * sums[1], green + weight * sums[2], blue + weight * sums[3])

        zero = jnp.zeros((rows, LANES), jnp.float32)
        depth, _, red, green, blue = lax.fori_loop(
            0, slices, advance, (zero, zero + 1.0, zero, zero, zero), unroll=2
        )
        out_ref[0, :, lanes] = red
        out_ref[1, :, lanes] = green
        out_ref[2, :, lanes] = blue
        out_ref[3, :, lanes] = depth


def render(front, params, matrices, own, two, odd, slices, rows):
    cols = own.shape[1]
    block = min(BLOCK, cols)

    def whole(m):
        return pl.BlockSpec(m.shape, lambda c: (0, 0))

    def columns(a):
        return pl.BlockSpec((a.shape[0], block), lambda c: (0, c))

    smem = pl.BlockSpec(memory_space=pltpu.SMEM)
    cells = slices * rows * cols
    return pl.pallas_call(
        lambda *refs: render_kernel(slices, rows, *refs),
        out_shape=jax.ShapeDtypeStruct((4, rows, cols), jnp.float32),
        grid=(cols // block,),
        in_specs=[smem, smem] + [whole(m) for m in matrices] + [columns(a) for a in (own, two, odd)],
        out_specs=pl.BlockSpec((4, rows, block), lambda c: (0, 0, c)),
        scratch_shapes=[pltpu.VMEM((slices * rows, block), jnp.float32)],
        compiler_params=pltpu.CompilerParams(vmem_limit_bytes=40 * 1024 * 1024),
        cost_estimate=pl.CostEstimate(flops=cells * 6000, bytes_accessed=cells * 6, transcendentals=cells * 9),
        name="render",
    )(front, params, *matrices, own, two, odd)


def pick(matrix, rows):
    return jnp.dot(matrix, rows, preferred_element_type=jnp.float32).astype(jnp.bfloat16)


def partial_image(two_cap, odd_cap, volume, local_shift, front, params):
    slices, rows, cols = volume.shape
    total = slices * rows
    target, far = plan(local_shift, rows)
    two_at = positions(far >= 2)
    odd_at = positions(far % 2 == 1)
    two_send = one_hot(two_at, two_cap)
    odd_own = one_hot(jnp.where(far == 1, odd_at, -1), odd_cap)
    two_index = jnp.arange(two_cap, dtype=jnp.int32)
    hop = jnp.where(far == 3, two_at, -1).reshape(1, -1)
    odd_two = jnp.dot(
        one_hot(odd_at, odd_cap),
        (hop.reshape(-1, 1) == two_index[None, :]).astype(jnp.bfloat16),
        preferred_element_type=jnp.float32,
    ).astype(jnp.bfloat16)
    source = jnp.arange(rows, dtype=jnp.int32)
    picks = target[:, None, :] == source[None, :, None]

    def by_target(values):
        return jnp.max(jnp.where(picks, values[:, None, :], -1), axis=2).reshape(-1, 1)

    flat = jnp.arange(total, dtype=jnp.int32).reshape(slices, rows)

    def place(values, count):
        return (by_target(values) == jnp.arange(count, dtype=jnp.int32)[None, :]).astype(jnp.bfloat16)

    matrices = (
        place(jnp.where(far == 0, flat, -1), total),
        place(jnp.where(far == 2, two_at, -1), two_cap),
        place(odd_at, odd_cap),
    )
    field = volume.reshape(total, cols)
    width = cols // CHUNKS
    parts = []
    for c in range(CHUNKS):
        own = field[:, c * width : (c + 1) * width]
        two = from_behind(pick(two_send, own), "lat", -2)
        relay = jnp.dot(odd_own, own, preferred_element_type=jnp.float32) + jnp.dot(
            odd_two, two, preferred_element_type=jnp.float32
        )
        odd = from_behind(relay.astype(jnp.bfloat16), "lat", -1)
        parts.append(render(front, params, matrices, own, two, odd, slices, rows))
    return jnp.concatenate(parts, axis=2)


def local(volume, shift_table, slab_order, centers, widths, extinct, colors):
    slabs = lax.axis_size("depth")
    slices, rows, cols = volume.shape
    total = slices * rows
    inv_depth = 1.0 / (slices * slabs)
    params = jnp.concatenate([centers[None], -widths[None], (extinct * inv_depth)[None], colors], axis=0)
    slab = lax.axis_index("depth")
    local_shift = lax.dynamic_slice_in_dim(shift_table, slab * slices, slices)
    two_cap, odd_cap = total * 11 // 16, total * 10 // 16
    over = jnp.zeros((), jnp.int32)
    _, all_far = plan(shift_table, rows)
    for s in range(slabs):
        far = all_far[s * slices : (s + 1) * slices]
        over = jnp.maximum(over, jnp.sum((far >= 2).astype(jnp.int32)) - two_cap)
        over = jnp.maximum(over, jnp.sum((far % 2 == 1).astype(jnp.int32)) - odd_cap)
    over = max_over(over.reshape(1, 1), "views")[0, 0]
    partial_value = lax.cond(
        over > 0,
        lambda *a: partial_image(total, total, *a),
        lambda *a: partial_image(two_cap, odd_cap, *a),
        volume,
        local_shift,
        slab_order,
        params,
    )
    own_cols = cols // slabs
    theirs = lax.dynamic_slice_in_dim(partial_value, (1 - slab) * own_cols, own_cols, 2)
    mine = lax.dynamic_slice_in_dim(partial_value, slab * own_cols, own_cols, 2)
    other = lax.ppermute(theirs, "depth", [(0, 1), (1, 0)])
    mine_first = slab_order[0, 0] == slab
    front = jnp.where(mine_first, mine, other)
    back = jnp.where(mine_first, other, mine)
    color = front[:3] + jnp.exp(-front[3])[None] * back[:3]
    opacity = 1.0 - jnp.exp(-(mine[3] + other[3]))
    return jnp.concatenate([color, opacity[None]], axis=0)


def solution(mesh):
    in_specs = (
        P(("views", "depth"), "lat", None),
        P("views"),
        P(("views", "lat"), None),
        P(),
        P(),
        P(),
        P(),
    )
    out_specs = P(None, ("views", "lat"), "depth")
    return jax.shard_map(local, mesh=mesh, in_specs=in_specs, out_specs=out_specs, check_vma=False)
```

time: 857 us -> 157 us (0.18)
  other arithmetic: 442 us -> 5.27 us
  waiting for transfers between devices: 265 us -> 28.3 us
  local copies, waits for them, and re-layouts: 112 us -> 3.6 us
  Pallas kernels: 0 us -> 57.8 us
  matrix products: 0 us -> 25.1 us
  starting transfers between devices: 14.9 us -> 29.6 us
  loops' own time: 11.7 us -> 0.83 us
    mul x16 -> x1, other arithmetic: 274 us -> 0.02 us  [local(): color = front[:3] + jnp.exp(-front[3])[None] * back[:3]]
    ppermute x3 -> x8, waiting for transfers between devices: 265 us -> 27.4 us  [from_behind(): return lax.ppermute(block, axis, route)]
    exp x9 -> x0, other arithmetic: 91 us -> none  [the longest x8 90.8 us: classify(): jnp.exp(-jnp.square(samples - centers[lobe_index]) * widths[lobe_index])]
    pallas_call x0 -> x4, Pallas kernels: none -> 57.8 us  [render(): pl.pallas_call(lambda *refs: render_kernel(slices, rows, *refs), out_shap...]
    exp x64 -> x0, local copies, waits for them, and re-layouts: 39.2 us -> none  [classify(): jnp.exp(-jnp.square(samples - centers[lobe_index]) * widths[lobe_index])]
    another operation x8 -> x0, other arithmetic: 37.4 us -> none  [advance(): inclusive = jnp.cumsum(optical, axis=0)]
    dot_general x0 -> x13, matrix products: none -> 25.1 us  [the longest x4 8.55 us: pick(): jnp.dot(matrix, rows, preferred_element_type=jnp.float32)]
    gather x8 -> x0, local copies, waits for them, and re-layouts: 16.5 us -> none  [take_rows(): return lax.dynamic_slice_in_dim(plane, offset, row_count, 0)]
  transfers between devices with their start and end apart: 3 -> 10, of which waited for: 3 -> 5; matrix products, arithmetic and copies ran while one was open for 0% -> 18% of each run, Pallas kernels for 0% -> 28%
where the time goes in v1:
time: 157 us; the launch traced here: 154 us
  Pallas kernels  57.8 us (37%)
  starting transfers between devices  29.6 us (19%)
  waiting for transfers between devices  28.3 us (18%)
  matrix products  25.1 us (16%)
  other arithmetic  5.27 us (3%)
  between operations  3.95 us (3%)
  local copies, waits for them, and re-layouts  3.6 us (2%)
    pallas_call x4, Pallas kernels, render(): pl.pallas_call(lambda *refs: render_kernel(slices, rows, *refs), out_shap...  57.8 us
    ppermute x8, waiting for transfers between devices, from_behind(): return lax.ppermute(block, axis, route)  27.4 us
    ppermute x8, starting transfers between devices, from_behind(): return lax.ppermute(block, axis, route)  26.6 us
    dot_general x4, matrix products, pick(): jnp.dot(matrix, rows, preferred_element_type=jnp.float32)  8.55 us
    dot_general x4, matrix products, partial_image(): jnp.dot(odd_own, own, preferred_element_type=jnp.float32)  7.71 us
    dot_general x4, matrix products, partial_image(): jnp.dot(odd_two, two, preferred_element_type=jnp.float32)  7.31 us
  transfers between devices with their start and end apart: 10, of which 5 were waited for; matrix products, arithmetic and copies ran while one was open for 18% of the time, Pallas kernels for 28%

profile of v1, /device:TPU:24, one launch (start us, length us, event | category | flops | bytes accessed | tf_op | source)
XLA Modules:
  0.0 154.4 jit_solution(11661393627222431518)
XLA Ops:
  0.0 0.7 add_select_fusion.16
  0.7 0.8 convert_reduce_fusion
  4.0 2.9 %collective-permute-start.16 = (s32[1,1]{1,0:T(1,128)}, s32[1,1]{1,0:T(1,128)}, u32[]{:S(2)}, u32[]{:S(2)}) collective-permute-start(s32[1,1]{1,0:T(1,128)} %bitcast.3), channel_id=1, source_target_pairs={{0,16},{16,0},{1,17},{17,1},{2,18},{18,2},{3,19},{19,3},{4,20},{20... | collective-permute-start | bytes 20 | tf_op jit(solution)/shard_map/ppermute | solution.py:24
  6.9 0.7 dynamic_slice.9
  7.6 0.7 multiply_bitcast_fusion
  8.3 0.7 pad_maximum_fusion.3
  9.7 142.2 %conditional.1 = (f32[4,16,2048]{2,1,0:T(8,128)S(1)}) conditional(s32[]{:T(128)} %bitcast.4, (s32[64]{0:T(128)S(1)}, bf16[64,16,2048]{2,1,0:T(8,128)(2,1)}, s32[1,2]{1,0:T(1,128)}, f32[6,8]{1,0:T(8,128)S(1)}) %tuple.11, (s32[64]{0:T(128)S(1)}, bf16[64,16,2048]{2,1,0:T(8,128)(2,1)}, s32[1,2]{1,0:T(1,128)}, f32[6,8]{1,0:T(8,128)S(1)}) %tuple.11), branch_computations={%region_4.14_spmd, %region_14.24_spmd} | conditional | flops 27640207360 | bytes 173310016 | solution.py:185
  9.8 0.1 select_reduce_fusion.5
  9.9 0.1 select_reduce_fusion.1
  10.1 0.1 copy.13
  10.7 3.1 %fusion.18 = bf16[704,512]{1,0:T(8,128)(2,1)} fusion(s32[1024]{0:T(1024)S(1)} %get-tuple-element.67, bf16[1024,2048]{1,0:T(8,128)(2,1)} %bitcast.29), kind=kOutput, calls=%fused_computation.29 | convolution fusion | flops 739278848 | bytes 1773568 | tf_op jit(solution)/shard_map/cond/branch_0_fun/dot_general | solution.py:121
  13.8 3.2 %collective-permute-start = (bf16[704,512]{1,0:T(8,128)(2,1)}, bf16[704,512]{1,0:T(8,128)(2,1)}, u32[]{:S(2)}, u32[]{:S(2)}) collective-permute-start(bf16[704,512]{1,0:T(8,128)(2,1)} %fusion.18), channel_id=1, source_target_pairs={{2,0},{3,1},{4,2},{5,3},{6,4},{7,5},{10,8},{11,9},{12,10},{13,11},... | collective-permute-start | bytes 2162696 | tf_op jit(solution)/shard_map/cond/branch_0_fun/ppermute | solution.py:16
  17.0 1.8 %fusion.19 = bf16[704,512]{1,0:T(8,128)(2,1)} fusion(s32[1024]{0:T(1024)S(1)} %get-tuple-element.67, bf16[1024,2048]{1,0:T(8,128)(2,1)S(1)} %bitcast.30), kind=kOutput, calls=%fused_computation.30 | convolution fusion | flops 739278848 | bytes 1773568 | tf_op jit(solution)/shard_map/cond/branch_0_fun/dot_general | solution.py:121
  18.8 2.4 %collective-permute-start.2 = (bf16[704,512]{1,0:T(8,128)(2,1)}, bf16[704,512]{1,0:T(8,128)(2,1)}, u32[]{:S(2)}, u32[]{:S(2)}) collective-permute-start(bf16[704,512]{1,0:T(8,128)(2,1)} %fusion.19), channel_id=1, source_target_pairs={{2,0},{3,1},{4,2},{5,3},{6,4},{7,5},{10,8},{11,9},{12,10},{13,11},... | collective-permute-start | bytes 2162696 | tf_op jit(solution)/shard_map/cond/branch_0_fun/ppermute | solution.py:16
  21.3 1.8 %fusion.20 = bf16[704,512]{1,0:T(8,128)(2,1)} fusion(s32[1024]{0:T(1024)S(1)} %get-tuple-element.67, bf16[1024,2048]{1,0:T(8,128)(2,1)S(1)} %bitcast.31), kind=kOutput, calls=%fused_computation.31 | convolution fusion | flops 739278848 | bytes 1773568 | tf_op jit(solution)/shard_map/cond/branch_0_fun/dot_general | solution.py:121
  23.1 2.4 %collective-permute-start.4 = (bf16[704,512]{1,0:T(8,128)(2,1)}, bf16[704,512]{1,0:T(8,128)(2,1)}, u32[]{:S(2)}, u32[]{:S(2)}) collective-permute-start(bf16[704,512]{1,0:T(8,128)(2,1)} %fusion.20), channel_id=1, source_target_pairs={{2,0},{3,1},{4,2},{5,3},{6,4},{7,5},{10,8},{11,9},{12,10},{13,11},... | collective-permute-start | bytes 2162696 | tf_op jit(solution)/shard_map/cond/branch_0_fun/ppermute | solution.py:16
  25.4 1.8 %fusion.21 = bf16[704,512]{1,0:T(8,128)(2,1)} fusion(s32[1024]{0:T(1024)S(1)} %get-tuple-element.67, bf16[1024,2048]{1,0:T(8,128)(2,1)S(1)} %bitcast.32), kind=kOutput, calls=%fused_computation.32 | convolution fusion | flops 739278848 | bytes 1773568 | tf_op jit(solution)/shard_map/cond/branch_0_fun/dot_general | solution.py:121
  27.2 2.1 %collective-permute-start.6 = (bf16[704,512]{1,0:T(8,128)(2,1)}, bf16[704,512]{1,0:T(8,128)(2,1)}, u32[]{:S(2)}, u32[]{:S(2)}) collective-permute-start(bf16[704,512]{1,0:T(8,128)(2,1)} %fusion.21), channel_id=1, source_target_pairs={{2,0},{3,1},{4,2},{5,3},{6,4},{7,5},{10,8},{11,9},{12,10},{13,11},... | collective-permute-start | bytes 2162696 | tf_op jit(solution)/shard_map/cond/branch_0_fun/ppermute | solution.py:16
  29.4 1.8 %fusion.130 = (bf16[1024,512]{1,0:T(8,128)(2,1)}, bf16[1024,512]{1,0:T(8,128)(2,1)S(1)}, bf16[1024,512]{1,0:T(8,128)(2,1)}, bf16[1024,512]{1,0:T(8,128)(2,1)}) fusion(bf16[1024,2048]{1,0:T(8,128)(2,1)S(1)} %bitcast.33), kind=kLoop, calls=%fused_computation.263 | loop fusion | bytes 8388608 | tf_op jit(solution)/shard_map/cond/branch_0_fun/slice | solution.py:159
  31.1 1.9 %fusion.10 = f32[640,512]{1,0:T(8,128)} fusion(s32[1024]{0:T(1024)S(1)} %get-tuple-element.68, bf16[1024,2048]{1,0:T(8,128)(2,1)S(1)} %bitcast.34), kind=kOutput, calls=%fused_computation.16 | convolution fusion | flops 671744000 | bytes 2363392 | tf_op jit(solution)/shard_map/cond/branch_0_fun/dot_general | solution.py:161
  33.1 1.9 %fusion.9 = f32[640,512]{1,0:T(8,128)} fusion(s32[1024]{0:T(1024)S(1)} %get-tuple-element.68, bf16[1024,2048]{1,0:T(8,128)(2,1)S(1)} %bitcast.35), kind=kOutput, calls=%fused_computation.15 | convolution fusion | flops 671744000 | bytes 2363392 | tf_op jit(solution)/shard_map/cond/branch_0_fun/dot_general | solution.py:161
  35.0 1.9 %fusion.8 = f32[640,512]{1,0:T(8,128)} fusion(s32[1024]{0:T(1024)S(1)} %get-tuple-element.68, bf16[1024,2048]{1,0:T(8,128)(2,1)S(1)} %bitcast.36), kind=kOutput, calls=%fused_computation.14 | convolution fusion | flops 671744000 | bytes 2363392 | tf_op jit(solution)/shard_map/cond/branch_0_fun/dot_general | solution.py:161
  36.9 1.9 %fusion.7 = f32[640,512]{1,0:T(8,128)} fusion(s32[1024]{0:T(1024)S(1)} %get-tuple-element.68, bf16[1024,2048]{1,0:T(8,128)(2,1)S(1)} %bitcast.37), kind=kOutput, calls=%fused_computation.13 | convolution fusion | flops 671744000 | bytes 2363392 | tf_op jit(solution)/shard_map/cond/branch_0_fun/dot_general | solution.py:161
  38.9 0.1 select_reduce_fusion
  39.0 0.1 copy.8
  39.1 0.4 fusion.refs_2_
  39.6 0.1 copy.9
  39.9 0.3 fusion.1.refs_3_
  40.2 1.5 fusion.13
  41.8 0.3 fusion.11.refs_4_
  42.1 1.9 %fusion.22 = bf16[640,512]{1,0:T(8,128)(2,1)S(1)} fusion(f32[640,512]{1,0:T(8,128)S(1)} %copy-done.13, bf16[640,704]{0,1:T(8,128)(2,1)S(1)} %fusion.13, bf16[704,512]{1,0:T(8,128)(2,1)} %collective-permute-done.refs_6_), kind=kOutput, calls=%fused_computation.33 | convolution fusion | flops 462028800 | bytes 3588096 | tf_op jit(solution)/shard_map/cond/branch_0_fun/dot_general | solution.py:161
  44.0 2.2 %collective-permute-start.1 = (bf16[640,512]{1,0:T(8,128)(2,1)S(1)}, bf16[640,512]{1,0:T(8,128)(2,1)S(1)}, u32[]{:S(2)}, u32[]{:S(2)}) collective-permute-start(bf16[640,512]{1,0:T(8,128)(2,1)S(1)} %fusion.22), channel_id=1, source_target_pairs={{1,0},{2,1},{3,2},{4,3},{5,4},{6,5},{7,6},{9,8},{10,9},{11,10},{12... | collective-permute-start | bytes 1966088 | tf_op jit(solution)/shard_map/cond/branch_0_fun/ppermute | solution.py:16
  46.2 2.3 %collective-permute-done.2.refs_6_ = bf16[704,512]{1,0:T(8,128)(2,1)} collective-permute-done((bf16[704,512]{1,0:T(8,128)(2,1)}, bf16[704,512]{1,0:T(8,128)(2,1)}, u32[]{:S(2)}, u32[]{:S(2)}) %collective-permute-start.2) | collective-permute-done | bytes 720928 | tf_op jit(solution)/shard_map/cond/branch_0_fun/ppermute | solution.py:16
  48.5 1.8 %fusion.23 = bf16[640,512]{1,0:T(8,128)(2,1)S(1)} fusion(f32[640,512]{1,0:T(8,128)S(1)} %copy-done.12, bf16[640,704]{0,1:T(8,128)(2,1)S(1)} %fusion.13, bf16[704,512]{1,0:T(8,128)(2,1)} %collective-permute-done.2.refs_6_), kind=kOutput, calls=%fused_computation.34 | convolution fusion | flops 462028800 | bytes 3588096 | tf_op jit(solution)/shard_map/cond/branch_0_fun/dot_general | solution.py:161
  50.3 5.5 %collective-permute-start.3 = (bf16[640,512]{1,0:T(8,128)(2,1)S(1)}, bf16[640,512]{1,0:T(8,128)(2,1)S(1)}, u32[]{:S(2)}, u32[]{:S(2)}) collective-permute-start(bf16[640,512]{1,0:T(8,128)(2,1)S(1)} %fusion.23), channel_id=1, source_target_pairs={{1,0},{2,1},{3,2},{4,3},{5,4},{6,5},{7,6},{9,8},{10,9},{11,10},{12... | collective-permute-start | bytes 1966088 | tf_op jit(solution)/shard_map/cond/branch_0_fun/ppermute | solution.py:16
  55.8 8.1 %collective-permute-done.4.refs_6_ = bf16[704,512]{1,0:T(8,128)(2,1)} collective-permute-done((bf16[704,512]{1,0:T(8,128)(2,1)}, bf16[704,512]{1,0:T(8,128)(2,1)}, u32[]{:S(2)}, u32[]{:S(2)}) %collective-permute-start.4) | collective-permute-done | bytes 720928 | tf_op jit(solution)/shard_map/cond/branch_0_fun/ppermute | solution.py:16
  64.0 1.8 %fusion.24 = bf16[640,512]{1,0:T(8,128)(2,1)S(1)} fusion(f32[640,512]{1,0:T(8,128)S(1)} %copy-done.11, bf16[640,704]{0,1:T(8,128)(2,1)S(1)} %fusion.13, bf16[704,512]{1,0:T(8,128)(2,1)} %collective-permute-done.4.refs_6_), kind=kOutput, calls=%fused_computation.35 | convolution fusion | flops 462028800 | bytes 3588096 | tf_op jit(solution)/shard_map/cond/branch_0_fun/dot_general | solution.py:161
  65.8 5.5 %collective-permute-start.5 = (bf16[640,512]{1,0:T(8,128)(2,1)S(1)}, bf16[640,512]{1,0:T(8,128)(2,1)S(1)}, u32[]{:S(2)}, u32[]{:S(2)}) collective-permute-start(bf16[640,512]{1,0:T(8,128)(2,1)S(1)} %fusion.24), channel_id=1, source_target_pairs={{1,0},{2,1},{3,2},{4,3},{5,4},{6,5},{7,6},{9,8},{10,9},{11,10},{12... | collective-permute-start | bytes 1966088 | tf_op jit(solution)/shard_map/cond/branch_0_fun/ppermute | solution.py:16
  71.3 8.1 %collective-permute-done.6.refs_6_ = bf16[704,512]{1,0:T(8,128)(2,1)} collective-permute-done((bf16[704,512]{1,0:T(8,128)(2,1)}, bf16[704,512]{1,0:T(8,128)(2,1)}, u32[]{:S(2)}, u32[]{:S(2)}) %collective-permute-start.6) | collective-permute-done | bytes 720928 | tf_op jit(solution)/shard_map/cond/branch_0_fun/ppermute | solution.py:16
  79.4 1.8 %fusion.25 = bf16[640,512]{1,0:T(8,128)(2,1)S(1)} fusion(f32[640,512]{1,0:T(8,128)S(1)} %copy-done.10, bf16[640,704]{0,1:T(8,128)(2,1)S(1)} %fusion.13, bf16[704,512]{1,0:T(8,128)(2,1)} %collective-permute-done.6.refs_6_), kind=kOutput, calls=%fused_computation.36 | convolution fusion | flops 462028800 | bytes 3588096 | tf_op jit(solution)/shard_map/cond/branch_0_fun/dot_general | solution.py:161
  81.2 3.3 %collective-permute-start.7 = (bf16[640,512]{1,0:T(8,128)(2,1)S(1)}, bf16[640,512]{1,0:T(8,128)(2,1)S(1)}, u32[]{:S(2)}, u32[]{:S(2)}) collective-permute-start(bf16[640,512]{1,0:T(8,128)(2,1)S(1)} %fusion.25), channel_id=1, source_target_pairs={{1,0},{2,1},{3,2},{4,3},{5,4},{6,5},{7,6},{9,8},{10,9},{11,10},{12... | collective-permute-start | bytes 1966088 | tf_op jit(solution)/shard_map/cond/branch_0_fun/ppermute | solution.py:16
  84.5 8.8 %collective-permute-done.1.refs_7_ = bf16[640,512]{1,0:T(8,128)(2,1)S(1)} collective-permute-done((bf16[640,512]{1,0:T(8,128)(2,1)S(1)}, bf16[640,512]{1,0:T(8,128)(2,1)S(1)}, u32[]{:S(2)}, u32[]{:S(2)}) %collective-permute-start.1) | collective-permute-done | bytes 655392 | tf_op jit(solution)/shard_map/cond/branch_0_fun/ppermute | solution.py:16
  93.4 14.5 %render.8 = f32[4,16,512]{2,1,0:T(8,128)S(1)} custom-call(s32[1,2]{1,0:T(1,128)S(1)} %copy-done.8, f32[6,8]{1,0:T(8,128)S(1)} %get-tuple-element.25.refs_1_, bf16[1024,1024]{1,0:T(8,128)(2,1)S(1)} %fusion.refs_2_, bf16[1024,704]{1,0:T(8,128)(2,1)S(1)} %fusion.1.refs_3_, bf16[1024,640]{1,0:T(8,128)(2,1)S(1)} %fusion.11.refs_4_, ...), custom_call_target="tpu_custom_call" | custom-call | flops 3145728000 | bytes 3145728 | tf_op jit(solution)/shard_map/cond/branch_0_fun/render/pallas_call | solution.py:107
  107.9 14.5 %render.9 = f32[4,16,512]{2,1,0:T(8,128)S(1)} custom-call(s32[1,2]{1,0:T(1,128)S(1)} %copy-done.8, f32[6,8]{1,0:T(8,128)S(1)} %get-tuple-element.25.refs_1_, bf16[1024,1024]{1,0:T(8,128)(2,1)S(1)} %fusion.refs_2_, bf16[1024,704]{1,0:T(8,128)(2,1)S(1)} %fusion.1.refs_3_, bf16[1024,640]{1,0:T(8,128)(2,1)S(1)} %fusion.11.refs_4_, ...), custom_call_target="tpu_custom_call" | custom-call | flops 3145728000 | bytes 3145728 | tf_op jit(solution)/shard_map/cond/branch_0_fun/render/pallas_call | solution.py:107
  122.4 14.4 %render.10 = f32[4,16,512]{2,1,0:T(8,128)S(1)} custom-call(s32[1,2]{1,0:T(1,128)S(1)} %copy-done.8, f32[6,8]{1,0:T(8,128)S(1)} %get-tuple-element.25.refs_1_, bf16[1024,1024]{1,0:T(8,128)(2,1)S(1)} %fusion.refs_2_, bf16[1024,704]{1,0:T(8,128)(2,1)S(1)} %fusion.1.refs_3_, bf16[1024,640]{1,0:T(8,128)(2,1)S(1)} %fusion.11.refs_4_, ...), custom_call_target="tpu_custom_call" | custom-call | flops 3145728000 | bytes 3145728 | tf_op jit(solution)/shard_map/cond/branch_0_fun/render/pallas_call | solution.py:107
  136.8 14.4 %render.11 = f32[4,16,512]{2,1,0:T(8,128)S(1)} custom-call(s32[1,2]{1,0:T(1,128)S(1)} %copy-done.8, f32[6,8]{1,0:T(8,128)S(1)} %get-tuple-element.25.refs_1_, bf16[1024,1024]{1,0:T(8,128)(2,1)S(1)} %fusion.refs_2_, bf16[1024,704]{1,0:T(8,128)(2,1)S(1)} %fusion.1.refs_3_, bf16[1024,640]{1,0:T(8,128)(2,1)S(1)} %fusion.11.refs_4_, ...), custom_call_target="tpu_custom_call" | custom-call | flops 3145728000 | bytes 3145728 | tf_op jit(solution)/shard_map/cond/branch_0_fun/render/pallas_call | solution.py:107
  152.6 0.9 collective-permute-done.17
  153.6 0.7 pad_maximum_fusion.2
  (47 shorter events, 1.3 us)
Async XLA Ops:
  4.0 5.0 %collective-permute-start.16 = (s32[1,1]{1,0:T(1,128)}, s32[1,1]{1,0:T(1,128)}, u32[]{:S(2)}, u32[]{:S(2)}) collective-permute-start(s32[1,1]{1,0:T(1,128)} %bitcast.3), channel_id=1, source_target_pairs={{0,16},{16,0},{1,17},{17,1},{2,18},{18,2},{3,19},{19,3},{4,20},{20... | collective-permute-start | bytes 20 | tf_op jit(solution)/shard_map/ppermute | solution.py:24
  10.6 6.4 %copy-start.6 = (bf16[64,16,2048]{2,1,0:T(8,128)(2,1)S(1)}, bf16[64,16,2048]{2,1,0:T(8,128)(2,1)}, u32[]{:S(2)}) copy-start(bf16[64,16,2048]{2,1,0:T(8,128)(2,1)} %get-tuple-element.27) | copy-start | bytes 12582916 | tf_op jit(solution)/shard_map/cond
  13.8 28.2 %collective-permute-start = (bf16[704,512]{1,0:T(8,128)(2,1)}, bf16[704,512]{1,0:T(8,128)(2,1)}, u32[]{:S(2)}, u32[]{:S(2)}) collective-permute-start(bf16[704,512]{1,0:T(8,128)(2,1)} %fusion.18), channel_id=1, source_target_pairs={{2,0},{3,1},{4,2},{5,3},{6,4},{7,5},{10,8},{11,9},{12,10},{13,11},... | collective-permute-start | bytes 2162696 | tf_op jit(solution)/shard_map/cond/branch_0_fun/ppermute | solution.py:16
  18.8 29.7 %collective-permute-start.2 = (bf16[704,512]{1,0:T(8,128)(2,1)}, bf16[704,512]{1,0:T(8,128)(2,1)}, u32[]{:S(2)}, u32[]{:S(2)}) collective-permute-start(bf16[704,512]{1,0:T(8,128)(2,1)} %fusion.19), channel_id=1, source_target_pairs={{2,0},{3,1},{4,2},{5,3},{6,4},{7,5},{10,8},{11,9},{12,10},{13,11},... | collective-permute-start | bytes 2162696 | tf_op jit(solution)/shard_map/cond/branch_0_fun/ppermute | solution.py:16
  23.1 40.9 %collective-permute-start.4 = (bf16[704,512]{1,0:T(8,128)(2,1)}, bf16[704,512]{1,0:T(8,128)(2,1)}, u32[]{:S(2)}, u32[]{:S(2)}) collective-permute-start(bf16[704,512]{1,0:T(8,128)(2,1)} %fusion.20), channel_id=1, source_target_pairs={{2,0},{3,1},{4,2},{5,3},{6,4},{7,5},{10,8},{11,9},{12,10},{13,11},... | collective-permute-start | bytes 2162696 | tf_op jit(solution)/shard_map/cond/branch_0_fun/ppermute | solution.py:16
  27.2 52.2 %collective-permute-start.6 = (bf16[704,512]{1,0:T(8,128)(2,1)}, bf16[704,512]{1,0:T(8,128)(2,1)}, u32[]{:S(2)}, u32[]{:S(2)}) collective-permute-start(bf16[704,512]{1,0:T(8,128)(2,1)} %fusion.21), channel_id=1, source_target_pairs={{2,0},{3,1},{4,2},{5,3},{6,4},{7,5},{10,8},{11,9},{12,10},{13,11},... | collective-permute-start | bytes 2162696 | tf_op jit(solution)/shard_map/cond/branch_0_fun/ppermute | solution.py:16
  40.2 1.8 %copy-start.13 = (f32[640,512]{1,0:T(8,128)S(1)}, f32[640,512]{1,0:T(8,128)}, u32[]{:S(2)}) copy-start(f32[640,512]{1,0:T(8,128)} %fusion.10) | copy-start | bytes 3932164 | tf_op jit(solution)/shard_map/cond
  41.7 6.8 %copy-start.12 = (f32[640,512]{1,0:T(8,128)S(1)}, f32[640,512]{1,0:T(8,128)}, u32[]{:S(2)}) copy-start(f32[640,512]{1,0:T(8,128)} %fusion.9) | copy-start | bytes 3932164 | tf_op jit(solution)/shard_map/cond
  44.0 20.0 %copy-start.11 = (f32[640,512]{1,0:T(8,128)S(1)}, f32[640,512]{1,0:T(8,128)}, u32[]{:S(2)}) copy-start(f32[640,512]{1,0:T(8,128)} %fusion.8) | copy-start | bytes 3932164 | tf_op jit(solution)/shard_map/cond
  44.0 49.4 %collective-permute-start.1 = (bf16[640,512]{1,0:T(8,128)(2,1)S(1)}, bf16[640,512]{1,0:T(8,128)(2,1)S(1)}, u32[]{:S(2)}, u32[]{:S(2)}) collective-permute-start(bf16[640,512]{1,0:T(8,128)(2,1)S(1)} %fusion.22), channel_id=1, source_target_pairs={{1,0},{2,1},{3,2},{4,3},{5,4},{6,5},{7,6},{9,8},{10,9},{11,10},{12... | collective-permute-start | bytes 1966088 | tf_op jit(solution)/shard_map/cond/branch_0_fun/ppermute | solution.py:16
  50.3 29.1 %copy-start.10 = (f32[640,512]{1,0:T(8,128)S(1)}, f32[640,512]{1,0:T(8,128)}, u32[]{:S(2)}) copy-start(f32[640,512]{1,0:T(8,128)} %fusion.7) | copy-start | bytes 3932164 | tf_op jit(solution)/shard_map/cond
  50.3 57.5 %collective-permute-start.3 = (bf16[640,512]{1,0:T(8,128)(2,1)S(1)}, bf16[640,512]{1,0:T(8,128)(2,1)S(1)}, u32[]{:S(2)}, u32[]{:S(2)}) collective-permute-start(bf16[640,512]{1,0:T(8,128)(2,1)S(1)} %fusion.23), channel_id=1, source_target_pairs={{1,0},{2,1},{3,2},{4,3},{5,4},{6,5},{7,6},{9,8},{10,9},{11,10},{12... | collective-permute-start | bytes 1966088 | tf_op jit(solution)/shard_map/cond/branch_0_fun/ppermute | solution.py:16
  65.8 27.6 %copy-start.4 = (bf16[1024,512]{1,0:T(8,128)(2,1)S(1)}, bf16[1024,512]{1,0:T(8,128)(2,1)}, u32[]{:S(2)}) copy-start(bf16[1024,512]{1,0:T(8,128)(2,1)} %get-tuple-element.62.refs_5_) | copy-start | bytes 3145732 | tf_op jit(solution)/shard_map/cond
  65.8 27.6 %copy-start.8 = (s32[1,2]{1,0:T(1,128)S(1)}, s32[1,2]{1,0:T(1,128)}, u32[]{:S(2)}) copy-start(s32[1,2]{1,0:T(1,128)} %get-tuple-element.24.refs_0_) | copy-start | bytes 28 | tf_op jit(solution)/shard_map/cond
  65.8 56.6 %collective-permute-start.5 = (bf16[640,512]{1,0:T(8,128)(2,1)S(1)}, bf16[640,512]{1,0:T(8,128)(2,1)S(1)}, u32[]{:S(2)}, u32[]{:S(2)}) collective-permute-start(bf16[640,512]{1,0:T(8,128)(2,1)S(1)} %fusion.24), channel_id=1, source_target_pairs={{1,0},{2,1},{3,2},{4,3},{5,4},{6,5},{7,6},{9,8},{10,9},{11,10},{12... | collective-permute-start | bytes 1966088 | tf_op jit(solution)/shard_map/cond/branch_0_fun/ppermute | solution.py:16
  81.2 55.6 %collective-permute-start.7 = (bf16[640,512]{1,0:T(8,128)(2,1)S(1)}, bf16[640,512]{1,0:T(8,128)(2,1)S(1)}, u32[]{:S(2)}, u32[]{:S(2)}) collective-permute-start(bf16[640,512]{1,0:T(8,128)(2,1)S(1)} %fusion.25), channel_id=1, source_target_pairs={{1,0},{2,1},{3,2},{4,3},{5,4},{6,5},{7,6},{9,8},{10,9},{11,10},{12... | collective-permute-start | bytes 1966088 | tf_op jit(solution)/shard_map/cond/branch_0_fun/ppermute | solution.py:16
  93.4 14.5 %copy-start.2 = (bf16[1024,512]{1,0:T(8,128)(2,1)S(1)}, bf16[1024,512]{1,0:T(8,128)(2,1)}, u32[]{:S(2)}) copy-start(bf16[1024,512]{1,0:T(8,128)(2,1)} %get-tuple-element.65.refs_5_) | copy-start | bytes 3145732 | tf_op jit(solution)/shard_map/cond
  107.9 14.5 %copy-start = (bf16[1024,512]{1,0:T(8,128)(2,1)S(1)}, bf16[1024,512]{1,0:T(8,128)(2,1)}, u32[]{:S(2)}) copy-start(bf16[1024,512]{1,0:T(8,128)(2,1)} %get-tuple-element.64.refs_5_) | copy-start | bytes 3145732 | tf_op jit(solution)/shard_map/cond
  151.9 1.6 %collective-permute-start.17 = (f32[4,16,1024]{2,1,0:T(8,128)S(1)}, f32[4,16,1024]{2,1,0:T(8,128)S(1)}, u32[]{:S(2)}, u32[]{:S(2)}) collective-permute-start(f32[4,16,1024]{2,1,0:T(8,128)S(1)} %constant_dynamic-slice_fusion), channel_id=1, source_target_pairs={{0,8},{8,0},{1,9},{9,1},{2,10},{10,2},{3,11},{11,3},{4,12},{12,4},... | collective-permute-start | bytes 786440 | tf_op jit(solution)/shard_map/ppermute | solution.py:197

commit v2 on v0

v2 whole, which is shorter than its diff:
```python
import math
import jax
import jax.numpy as jnp
from jax import lax
from jax.experimental import pallas as pl
from jax.experimental.pallas import tpu as pltpu
from jax.sharding import PartitionSpec as P

CHUNKS = 4
LANES = 128


def along_lat(block, distance):
    devices = range(lax.axis_size("lat"))
    route = [(i, i + distance) for i in devices if i + distance in devices]
    return lax.ppermute(block, "lat", route)


def max_over(value, axis):
    size = lax.axis_size(axis)
    best = value
    for step in range(1, size):
        route = [(i, (i + step) % size) for i in range(size)]
        best = jnp.maximum(best, lax.ppermute(value, axis, route))
    return best


def positions(wanted):
    slices, rows = wanted.shape
    ones = wanted.astype(jnp.int32)
    z = jnp.arange(slices, dtype=jnp.int32)
    counts = jnp.sum(ones, axis=1)
    base = jnp.sum(jnp.where(z[None, :] < z[:, None], counts[None, :], 0), axis=1)
    r = jnp.arange(rows, dtype=jnp.int32)
    rank = jnp.sum(jnp.where(r[None, :, None] > r[None, None, :], ones[:, None, :], 0), axis=2)
    return jnp.where(wanted, base[:, None] + rank, -1)


def plan(shift, rows):
    source = jnp.arange(rows, dtype=jnp.int32)[None, :]
    target = (source - shift[:, None]) % rows
    far = (target + shift[:, None]) // rows
    return target, far


def tables(shift, rows, caps):
    slices = shift.shape[0]
    target, far = plan(shift, rows)
    flat = jnp.arange(slices * rows, dtype=jnp.int32).reshape(slices, rows)
    r = jnp.arange(rows, dtype=jnp.int32)
    hits = target[:, None, :] == r[None, :, None]

    def pack(place, count):
        return (place.reshape(1, -1) == jnp.arange(count, dtype=jnp.int32)[:, None]).astype(jnp.bfloat16)

    def unpack(place, count):
        there = jnp.max(jnp.where(hits, place[:, None, :], -1), axis=2).reshape(-1, 1)
        return (there == jnp.arange(count, dtype=jnp.int32)[None, :]).astype(jnp.bfloat16)

    places = [positions(far == f) for f in (0, 2, 3)]
    packs = [pack(p, c) for p, c in zip(places, caps)]
    unpacks = [unpack(jnp.where(far == f, flat, -1), slices * rows) for f in (1, 0)]
    unpacks += [unpack(p, c) for p, c in zip(places, caps)]
    return packs, unpacks


def render_kernel(
    slices, rows, last_lat, front_ref, shift_ref, par_ref, own_m, top_m, up_m, one_m, two_m, own, up, one, two, out_ref, cells
):
    lobes = par_ref.shape[1]
    tile = 256
    lat = lax.axis_index("lat")

    def classify(samples):
        sums = None
        for k in range(lobes):
            off = samples - par_ref[0, k]
            lobe = jnp.exp2(off * off * par_ref[1, k])
            terms = [par_ref[2 + j, k] * lobe for j in range(4)]
            sums = terms if sums is None else [a + b for a, b in zip(sums, terms)]
        return tuple(sums)

    def fill(pairs):
        @pl.loop(0, cells.shape[0], step=tile)
        def _(start):
            at = pl.ds(pl.multiple_of(start, tile), tile)
            total = None
            for m, rows_ref in pairs:
                term = jnp.dot(m[at, :], rows_ref[...], preferred_element_type=jnp.float32)
                total = term if total is None else total + term
            cells[at, :] = total

    def cast(band, limit):
        forward = front_ref[0, band] == 0
        for part in range(out_ref.shape[3] // LANES):
            lanes = slice(part * LANES, (part + 1) * LANES)
            zero = jnp.zeros((rows, LANES), jnp.float32)
            empty = None if limit is None else classify(zero)

            def advance(i, carry):
                depth, clear, red, green, blue = carry
                z = jnp.where(forward, i, slices - 1 - i)

                def filled():
                    return classify(cells[pl.ds(pl.multiple_of(z * rows, rows), rows), lanes])

                if limit is None:
                    sums = filled()
                else:
                    sums = lax.cond(shift_ref[0, z] >= limit, lambda: empty, filled)
                depth = depth + sums[0]
                after = jnp.exp2(-depth)
                weight = clear - after
                return (depth, after, red + weight * sums[1], green + weight * sums[2], blue + weight * sums[3])

            depth, _, red, green, blue = lax.fori_loop(
                0, slices, advance, (zero, zero + 1.0, zero, zero, zero), unroll=2 if limit is None else 1
            )
            out_ref[band, 0, :, lanes] = red
            out_ref[band, 1, :, lanes] = green
            out_ref[band, 2, :, lanes] = blue
            out_ref[band, 3, :, lanes] = depth

    fill([(own_m, own), (up_m, up), (one_m, one), (two_m, two)])

    @pl.when(lat != last_lat)
    def _():
        cast(0, None)
        out_ref[1] = jnp.zeros(out_ref.shape[1:], jnp.float32)

    @pl.when(lat == last_lat)
    def _():
        cast(0, 2 * rows)
        fill([(top_m, own)])
        cast(1, rows)


def render(front, shift, params, unpacks, field, up, one, two, chunk, slabs):
    slices = shift.shape[1]
    total, cols = field.shape
    rows = total // slices
    block = cols // slabs // CHUNKS
    stride = cols // slabs // block

    def whole(m):
        return pl.BlockSpec(m.shape, lambda c: (0, 0))

    def columns(a):
        return pl.BlockSpec((a.shape[0], block), lambda c: (0, c))

    smem = pl.BlockSpec(memory_space=pltpu.SMEM)
    cells = total * block * slabs
    last = lax.axis_size("lat") - 1
    return pl.pallas_call(
        lambda *refs: render_kernel(slices, rows, last, *refs),
        out_shape=jax.ShapeDtypeStruct((2, 4, rows, block * slabs), jnp.float32),
        grid=(slabs,),
        in_specs=[smem] * 3
        + [whole(m) for m in unpacks]
        + [pl.BlockSpec((total, block), lambda c: (0, c * stride + chunk))]
        + [columns(a) for a in (up, one, two)],
        out_specs=pl.BlockSpec((2, 4, rows, block), lambda c: (0, 0, 0, c)),
        scratch_shapes=[pltpu.VMEM((total, block), jnp.float32)],
        compiler_params=pltpu.CompilerParams(vmem_limit_bytes=48 * 1024 * 1024),
        cost_estimate=pl.CostEstimate(flops=cells * 24000, bytes_accessed=cells * 6, transcendentals=cells * 9),
        name="render",
    )(front, shift, params, *unpacks, field, up, one, two)


def pick(matrix, rows):
    return jnp.dot(matrix, rows, preferred_element_type=jnp.float32).astype(jnp.bfloat16)


def images(packs, unpacks, field, shift, orders, params):
    slabs = lax.axis_size("depth")
    slab = lax.axis_index("depth")
    last = lax.axis_index("lat") == lax.axis_size("lat") - 1
    total, cols = field.shape
    width = cols // slabs // CHUNKS
    front = orders[:, :1].T
    arrived = []
    for c in range(CHUNKS):
        own = jnp.concatenate(
            [field[:, s * (cols // slabs) + c * width :][:, :width] for s in range(slabs)], axis=1
        )
        arrived.append([along_lat(pick(m, own), d) for m, d in zip(packs, (1, -1, -2))])
    out = []
    mine_first = (orders[:, 0] == slab)[:, None, None, None]
    for c in range(CHUNKS):
        part = render(front, shift[None], params, unpacks, field, *arrived[c], c, slabs)
        theirs = lax.dynamic_slice_in_dim(part, (1 - slab) * width, width, 3)
        mine = lax.dynamic_slice_in_dim(part, slab * width, width, 3)
        other = lax.ppermute(theirs, "depth", [(0, 1), (1, 0)])
        near = jnp.where(mine_first, mine, other)
        behind = jnp.where(mine_first, other, mine)
        color = near[:, :3] + jnp.exp2(-near[:, 3:]) * behind[:, :3]
        opacity = 1.0 - jnp.exp2(-(mine[:, 3:] + other[:, 3:]))
        bands = jnp.concatenate([color, opacity], axis=1)
        out.append(jnp.where(last, bands[1], along_lat(bands[0], -1)))
    return jnp.concatenate(out, axis=2)


def local(volume, shift_table, slab_order, centers, widths, extinct, colors):
    slabs = lax.axis_size("depth")
    slices, rows, cols = volume.shape
    total = slices * rows
    log2e = math.log2(math.e)
    inv_depth = log2e / (slices * slabs)
    params = jnp.concatenate(
        [centers[None], (widths * -log2e)[None], (extinct * inv_depth)[None], colors], axis=0
    )
    slab = lax.axis_index("depth")
    shift = lax.dynamic_slice_in_dim(shift_table, slab * slices, slices)
    orders = jnp.concatenate([along_lat(slab_order, 1), slab_order], axis=0)
    caps = (total * 5 // 16, total * 15 // 32, total * 5 // 16)
    full = (total,) * 3
    over = jnp.zeros((), jnp.int32)
    _, all_far = plan(shift_table, rows)
    for s in range(slabs):
        far = all_far[s * slices : (s + 1) * slices]
        for f, cap in zip((0, 2, 3), caps):
            over = jnp.maximum(over, jnp.sum((far == f).astype(jnp.int32)) - cap)
    over = max_over(over.reshape(1, 1), "views")[0, 0]
    packs, unpacks = tables(shift, rows, caps)
    field = volume.reshape(total, cols)
    return lax.cond(
        over > 0,
        lambda p, u, f, s, *a: images(*tables(s, rows, full), f, s, *a),
        images,
        packs,
        unpacks,
        field,
        shift,
        orders,
        params,
    )


def solution(mesh):
    in_specs = (
        P(("views", "depth"), "lat", None),
        P("views"),
        P(("views", "lat"), None),
        P(),
        P(),
        P(),
        P(),
    )
    out_specs = P(None, ("views", "lat"), "depth")
    return jax.shard_map(local, mesh=mesh, in_specs=in_specs, out_specs=out_specs, check_vma=False)
```

time: 857 us -> 189 us (0.22)
  the two profiles are of different devices: /device:TPU:24 before, /device:TPU:27 now
where the time goes in v2:
time: 189 us; the launch traced here: 188 us
  starting transfers between devices  67.5 us (36%)
  Pallas kernels  55.6 us (29%)
  waiting for transfers between devices  25.7 us (14%)
  matrix products  17.3 us (9%)
  other arithmetic  9.31 us (5%)
  local copies, waits for them, and re-layouts  6.65 us (4%)
  between operations  4.61 us (2%)
    ppermute x17, starting transfers between devices, along_lat(): return lax.ppermute(block, 'lat', route)  62.9 us
    pallas_call x4, Pallas kernels, render(): pl.pallas_call(lambda *refs: render_kernel(slices, rows, last, *refs), ou...  55.6 us
    ppermute x17, waiting for transfers between devices, along_lat(): return lax.ppermute(block, 'lat', route)  24.5 us
    dot_general x12, matrix products, pick(): jnp.dot(matrix, rows, preferred_element_type=jnp.float32)  17.3 us
    convert_element_type x5, other arithmetic, unpack(): (there == jnp.arange(count, dtype=jnp.int32)[None, :]).astype(jnp.bfloat16)  5.93 us
  transfers between devices with their start and end apart: 22, of which 5 were waited for; matrix products, arithmetic and copies ran while one was open for 14% of the time, Pallas kernels for 30%

profile of v2, /device:TPU:27, one launch (start us, length us, event | category | flops | bytes accessed | tf_op | source)
XLA Modules:
  0.0 187.7 jit_solution(12213110997091989779)
XLA Ops:
  0.0 0.7 copy.23
  0.7 3.1 %collective-permute-start.41 = (s32[1,2]{0,1:T(2,128)S(1)}, s32[1,2]{0,1:T(2,128)S(1)}, u32[]{:S(2)}, u32[]{:S(2)}) collective-permute-start(s32[1,2]{0,1:T(2,128)S(1)} %copy.23), channel_id=1, source_target_pairs={{0,1},{1,2},{2,3},{3,4},{4,5},{5,6},{6,7},{8,9},{9,10},{10,11},{11... | collective-permute-start | bytes 32 | tf_op jit(solution)/shard_map/ppermute | solution.py:16
  4.6 0.8 convert_reduce_fusion
  9.2 1.0 collective-permute-start.40
  11.8 1.8 fusion.199
  13.7 1.7 fusion.200
  16.0 1.1 fusion.203
  17.3 1.1 fusion.204
  20.5 166.5 %conditional.1 = (f32[4,16,1024]{2,1,0:T(8,128)S(1)}) conditional(s32[]{:T(128)} %bitcast.43, (s32[2,2]{0,1:T(2,128)S(1)}, s32[64]{0:T(128)S(1)}, bf16[1024,2048]{1,0:T(8,128)(2,1)}, bf16[320,1024]{1,0:T(8,128)(2,1)S(1)}, bf16[480,1024]{1,0:T(8,128)(2,1)S(1)}, /*index=5*/bf16[320,1024]{1,0:T(8,128)(2,1)S(1)}, f32[6,8]{1,0:T(8,128)S(1)}, ...), branch_computations={%region_20.21_spmd, %region_21.36_spmd} | conditional | flops 63272546304 | bytes 143009408 | solution.py:226
  20.5 2.8 %fusion.232 = (bf16[1024,256]{1,0:T(8,128)(2,1)S(1)}, bf16[1024,256]{1,0:T(8,128)(2,1)S(1)}, bf16[1024,256]{1,0:T(8,128)(2,1)S(1)}, bf16[1024,256]{1,0:T(8,128)(...) fusion(bf16[1024,2048]{1,0:T(8,128)(2,1)} %get-tuple-element.48, ...), kind=kLoop, calls=%fused_computation.442 | loop fusion | bytes 8388608 | tf_op jit(solution)/shard_map/cond/branch_0_fun/slice | solution.py:184
  23.4 1.3 fusion.5
  24.7 2.1 %collective-permute-start.22 = (bf16[320,512]{1,0:T(8,128)(2,1)}, bf16[320,512]{1,0:T(8,128)(2,1)S(1)}, u32[]{:S(2)}, u32[]{:S(2)}) collective-permute-start(bf16[320,512]{1,0:T(8,128)(2,1)} %fusion.5), channel_id=1, source_target_pairs={{2,0},{3,1},{4,2},{5,3},{6,4},{7,5},{10,8},{11,9},{12,10},{13,11},... | collective-permute-start | bytes 983048 | tf_op jit(solution)/shard_map/cond/branch_0_fun/ppermute | solution.py:16
  26.7 1.5 fusion
  28.2 3.0 %collective-permute-start.21 = (bf16[480,512]{1,0:T(8,128)(2,1)}, bf16[480,512]{1,0:T(8,128)(2,1)S(1)}, u32[]{:S(2)}, u32[]{:S(2)}) collective-permute-start(bf16[480,512]{1,0:T(8,128)(2,1)} %fusion), channel_id=1, source_target_pairs={{1,0},{2,1},{3,2},{4,3},{5,4},{6,5},{7,6},{9,8},{10,9},{11,10},{12... | collective-permute-start | bytes 1474568 | tf_op jit(solution)/shard_map/cond/branch_0_fun/ppermute | solution.py:16
  31.2 1.2 fusion.4
  32.5 2.3 %collective-permute-start.20 = (bf16[320,512]{1,0:T(8,128)(2,1)}, bf16[320,512]{1,0:T(8,128)(2,1)S(1)}, u32[]{:S(2)}, u32[]{:S(2)}) collective-permute-start(bf16[320,512]{1,0:T(8,128)(2,1)} %fusion.4), channel_id=1, source_target_pairs={{0,1},{1,2},{2,3},{3,4},{4,5},{5,6},{6,7},{8,9},{9,10},{10,11},{11... | collective-permute-start | bytes 983048 | tf_op jit(solution)/shard_map/cond/branch_0_fun/ppermute | solution.py:16
  34.7 1.5 fusion.1
  36.2 3.9 %collective-permute-start.26 = (bf16[480,512]{1,0:T(8,128)(2,1)}, bf16[480,512]{1,0:T(8,128)(2,1)S(1)}, u32[]{:S(2)}, u32[]{:S(2)}) collective-permute-start(bf16[480,512]{1,0:T(8,128)(2,1)} %fusion.1), channel_id=1, source_target_pairs={{1,0},{2,1},{3,2},{4,3},{5,4},{6,5},{7,6},{9,8},{10,9},{11,10},{12... | collective-permute-start | bytes 1474568 | tf_op jit(solution)/shard_map/cond/branch_0_fun/ppermute | solution.py:16
  40.1 1.2 fusion.6
  41.3 1.9 %collective-permute-start.25 = (bf16[320,512]{1,0:T(8,128)(2,1)}, bf16[320,512]{1,0:T(8,128)(2,1)S(1)}, u32[]{:S(2)}, u32[]{:S(2)}) collective-permute-start(bf16[320,512]{1,0:T(8,128)(2,1)} %fusion.6), channel_id=1, source_target_pairs={{0,1},{1,2},{2,3},{3,4},{4,5},{5,6},{6,7},{8,9},{9,10},{10,11},{11... | collective-permute-start | bytes 983048 | tf_op jit(solution)/shard_map/cond/branch_0_fun/ppermute | solution.py:16
  43.3 1.2 fusion.7
  44.5 1.5 fusion.2
  46.0 1.2 fusion.8
  47.2 1.2 fusion.9
  48.4 1.3 fusion.11
  49.7 1.3 fusion.10
  51.0 3.0 %fusion.3 = bf16[480,512]{1,0:T(8,128)(2,1)} fusion(bf16[480,1024]{1,0:T(8,128)(2,1)} %copy-done.4, bf16[1024,256]{1,0:T(8,128)(2,1)S(1)} %get-tuple-element.102, bf16[1024,256]{1,0:T(8,128)(2,1)} %copy-done.9), kind=kOutput, calls=%fused_computation.7 | convolution fusion | flops 505659392 | bytes 2523136 | tf_op jit(solution)/shard_map/cond/branch_0_fun/dot_general | solution.py:171
  53.9 2.2 %collective-permute-start.27 = (bf16[320,512]{1,0:T(8,128)(2,1)S(1)}, bf16[320,512]{1,0:T(8,128)(2,1)S(1)}, u32[]{:S(2)}, u32[]{:S(2)}) collective-permute-start(bf16[320,512]{1,0:T(8,128)(2,1)S(1)} %copy-done.19), channel_id=1, source_target_pairs={{2,0},{3,1},{4,2},{5,3},{6,4},{7,5},{10,8},{11,9},{12,10},{13,11},... | collective-permute-start | bytes 983048 | tf_op jit(solution)/shard_map/cond/branch_0_fun/ppermute | solution.py:16
  56.1 8.8 %collective-permute-start.31 = (bf16[480,512]{1,0:T(8,128)(2,1)}, bf16[480,512]{1,0:T(8,128)(2,1)S(1)}, u32[]{:S(2)}, u32[]{:S(2)}) collective-permute-start(bf16[480,512]{1,0:T(8,128)(2,1)} %fusion.2), channel_id=1, source_target_pairs={{1,0},{2,1},{3,2},{4,3},{5,4},{6,5},{7,6},{9,8},{10,9},{11,10},{12... | collective-permute-start | bytes 1474568 | tf_op jit(solution)/shard_map/cond/branch_0_fun/ppermute | solution.py:16
  65.0 1.9 %collective-permute-start.30 = (bf16[320,512]{1,0:T(8,128)(2,1)}, bf16[320,512]{1,0:T(8,128)(2,1)S(1)}, u32[]{:S(2)}, u32[]{:S(2)}) collective-permute-start(bf16[320,512]{1,0:T(8,128)(2,1)} %fusion.8), channel_id=1, source_target_pairs={{0,1},{1,2},{2,3},{3,4},{4,5},{5,6},{6,7},{8,9},{9,10},{10,11},{11... | collective-permute-start | bytes 983048 | tf_op jit(solution)/shard_map/cond/branch_0_fun/ppermute | solution.py:16
  67.0 15.4 %render.8 = f32[2,4,16,512]{3,2,1,0:T(8,128)S(1)} custom-call(s32[1,2]{1,0:T(1,128)S(1)} %slice_bitcast_fusion.refs_0_, s32[1,64]{1,0:T(1,128)S(1)} %bitcast.120, f32[6,8]{1,0:T(8,128)S(1)} %get-tuple-element.42.refs_2_, bf16[1024,1024]{1,0:T(8,128)(2,1)} %get-tuple-element.43.refs_3_, bf16[1024,1024]{1,0:T(8,128)(2,1)} %get-tuple-element.44.refs_4_, ...), custom_call_target="tpu_custom_call" | custom-call | flops 12582912000 | bytes 3145728 | tf_op jit(solution)/shard_map/cond/branch_0_fun/render/pallas_call | solution.py:154
  82.4 2.3 %collective-permute-start.32 = (bf16[320,512]{1,0:T(8,128)(2,1)S(1)}, bf16[320,512]{1,0:T(8,128)(2,1)S(1)}, u32[]{:S(2)}, u32[]{:S(2)}) collective-permute-start(bf16[320,512]{1,0:T(8,128)(2,1)S(1)} %copy-done.18), channel_id=1, source_target_pairs={{2,0},{3,1},{4,2},{5,3},{6,4},{7,5},{10,8},{11,9},{12,10},{13,11},... | collective-permute-start | bytes 983048 | tf_op jit(solution)/shard_map/cond/branch_0_fun/ppermute | solution.py:16
  84.8 2.1 %collective-permute-start.37 = (bf16[320,512]{1,0:T(8,128)(2,1)S(1)}, bf16[320,512]{1,0:T(8,128)(2,1)S(1)}, u32[]{:S(2)}, u32[]{:S(2)}) collective-permute-start(bf16[320,512]{1,0:T(8,128)(2,1)S(1)} %copy-done.17), channel_id=1, source_target_pairs={{2,0},{3,1},{4,2},{5,3},{6,4},{7,5},{10,8},{11,9},{12,10},{13,11},... | collective-permute-start | bytes 983048 | tf_op jit(solution)/shard_map/cond/branch_0_fun/ppermute | solution.py:16
  86.9 4.2 %collective-permute-start.36 = (bf16[480,512]{1,0:T(8,128)(2,1)}, bf16[480,512]{1,0:T(8,128)(2,1)S(1)}, u32[]{:S(2)}, u32[]{:S(2)}) collective-permute-start(bf16[480,512]{1,0:T(8,128)(2,1)} %fusion.3), channel_id=1, source_target_pairs={{1,0},{2,1},{3,2},{4,3},{5,4},{6,5},{7,6},{9,8},{10,9},{11,10},{12... | collective-permute-start | bytes 1474568 | tf_op jit(solution)/shard_map/cond/branch_0_fun/ppermute | solution.py:16
  91.1 13.4 %render.9 = f32[2,4,16,512]{3,2,1,0:T(8,128)S(1)} custom-call(s32[1,2]{1,0:T(1,128)S(1)} %slice_bitcast_fusion.refs_0_, s32[1,64]{1,0:T(1,128)S(1)} %bitcast.121, f32[6,8]{1,0:T(8,128)S(1)} %get-tuple-element.42.refs_2_, bf16[1024,1024]{1,0:T(8,128)(2,1)S(1)} %copy-done.2, bf16[1024,1024]{1,0:T(8,128)(2,1)S(1)} %copy-done.3, ...), custom_call_target="tpu_custom_call" | custom-call | flops 12582912000 | bytes 3145728 | tf_op jit(solution)/shard_map/cond/branch_0_fun/render/pallas_call | solution.py:154
  104.6 17.5 %collective-permute-start.35 = (bf16[320,512]{1,0:T(8,128)(2,1)S(1)}, bf16[320,512]{1,0:T(8,128)(2,1)S(1)}, u32[]{:S(2)}, u32[]{:S(2)}) collective-permute-start(bf16[320,512]{1,0:T(8,128)(2,1)S(1)} %copy-done.16), channel_id=1, source_target_pairs={{0,1},{1,2},{2,3},{3,4},{4,5},{5,6},{6,7},{8,9},{9,10},{10,11},{11... | collective-permute-start | bytes 983048 | tf_op jit(solution)/shard_map/cond/branch_0_fun/ppermute | solution.py:16
  122.0 2.8 %collective-permute-start.23 = (f32[2,4,16,256]{3,2,1,0:T(8,128)S(1)}, f32[2,4,16,256]{3,2,1,0:T(8,128)S(1)}, u32[]{:S(2)}, u32[]{:S(2)}) collective-permute-start(f32[2,4,16,256]{3,2,1,0:T(8,128)S(1)} %constant_dynamic-slice_fusion.3), channel_id=1, source_target_pairs={{0,8},{8,0},{1,9},{9,1},{2,10},{10,2},{3,11},{11,3},{4,12},{12,4},... | collective-permute-start | bytes 393224 | tf_op jit(solution)/shard_map/cond/branch_0_fun/ppermute | solution.py:193
  124.9 13.4 %render.10 = f32[2,4,16,512]{3,2,1,0:T(8,128)S(1)} custom-call(s32[1,2]{1,0:T(1,128)S(1)} %slice_bitcast_fusion.refs_0_, s32[1,64]{1,0:T(1,128)S(1)} %bitcast.122, f32[6,8]{1,0:T(8,128)S(1)} %get-tuple-element.42.refs_2_, bf16[1024,1024]{1,0:T(8,128)(2,1)S(1)} %copy-done.2, bf16[1024,1024]{1,0:T(8,128)(2,1)S(1)} %copy-done.3, ...), custom_call_target="tpu_custom_call" | custom-call | flops 12582912000 | bytes 3145728 | tf_op jit(solution)/shard_map/cond/branch_0_fun/render/pallas_call | solution.py:154
  138.9 13.4 %render.11 = f32[2,4,16,512]{3,2,1,0:T(8,128)S(1)} custom-call(s32[1,2]{1,0:T(1,128)S(1)} %slice_bitcast_fusion.refs_0_, s32[1,64]{1,0:T(1,128)S(1)} %bitcast.123, f32[6,8]{1,0:T(8,128)S(1)} %get-tuple-element.42.refs_2_, bf16[1024,1024]{1,0:T(8,128)(2,1)S(1)} %copy-done.2, bf16[1024,1024]{1,0:T(8,128)(2,1)S(1)} %copy-done.3, ...), custom_call_target="tpu_custom_call" | custom-call | flops 12582912000 | bytes 3145728 | tf_op jit(solution)/shard_map/cond/branch_0_fun/render/pallas_call | solution.py:154
  152.5 1.2 collective-permute-done.38
  154.1 1.9 %collective-permute-start.24 = (f32[4,16,256]{2,1,0:T(8,128)S(1)}, f32[4,16,256]{2,1,0:T(8,128)S(1)}, u32[]{:S(2)}, u32[]{:S(2)}) collective-permute-start(f32[4,16,256]{2,1,0:T(8,128)S(1)} %fusion.35), channel_id=1, source_target_pairs={{1,0},{2,1},{3,2},{4,3},{5,4},{6,5},{7,6},{9,8},{10,9},{11,10},{12... | collective-permute-start | bytes 196616 | tf_op jit(solution)/shard_map/cond/branch_0_fun/ppermute | solution.py:16
  156.1 1.9 %collective-permute-start.29 = (f32[4,16,256]{2,1,0:T(8,128)S(1)}, f32[4,16,256]{2,1,0:T(8,128)S(1)}, u32[]{:S(2)}, u32[]{:S(2)}) collective-permute-start(f32[4,16,256]{2,1,0:T(8,128)S(1)} %fusion.34), channel_id=1, source_target_pairs={{1,0},{2,1},{3,2},{4,3},{5,4},{6,5},{7,6},{9,8},{10,9},{11,10},{12... | collective-permute-start | bytes 196616 | tf_op jit(solution)/shard_map/cond/branch_0_fun/ppermute | solution.py:16
  158.1 1.9 %collective-permute-start.34 = (f32[4,16,256]{2,1,0:T(8,128)S(1)}, f32[4,16,256]{2,1,0:T(8,128)S(1)}, u32[]{:S(2)}, u32[]{:S(2)}) collective-permute-start(f32[4,16,256]{2,1,0:T(8,128)S(1)} %fusion.33), channel_id=1, source_target_pairs={{1,0},{2,1},{3,2},{4,3},{5,4},{6,5},{7,6},{9,8},{10,9},{11,10},{12... | collective-permute-start | bytes 196616 | tf_op jit(solution)/shard_map/cond/branch_0_fun/ppermute | solution.py:16
  160.1 1.9 %collective-permute-start.39 = (f32[4,16,256]{2,1,0:T(8,128)S(1)}, f32[4,16,256]{2,1,0:T(8,128)S(1)}, u32[]{:S(2)}, u32[]{:S(2)}) collective-permute-start(f32[4,16,256]{2,1,0:T(8,128)S(1)} %fusion.32), channel_id=1, source_target_pairs={{1,0},{2,1},{3,2},{4,3},{5,4},{6,5},{7,6},{9,8},{10,9},{11,10},{12... | collective-permute-start | bytes 196616 | tf_op jit(solution)/shard_map/cond/branch_0_fun/ppermute | solution.py:16
  162.0 20.1 %collective-permute-done.24 = f32[4,16,256]{2,1,0:T(8,128)S(1)} collective-permute-done((f32[4,16,256]{2,1,0:T(8,128)S(1)}, f32[4,16,256]{2,1,0:T(8,128)S(1)}, u32[]{:S(2)}, u32[]{:S(2)}) %collective-permute-start.24) | collective-permute-done | bytes 65568 | tf_op jit(solution)/shard_map/cond/branch_0_fun/ppermute | solution.py:16
  182.1 1.4 collective-permute-done.29
  183.6 1.5 collective-permute-done.34
  185.0 1.4 collective-permute-done.39
  (114 shorter events, 6.7 us)
Async XLA Ops:
  0.7 19.7 %collective-permute-start.41 = (s32[1,2]{0,1:T(2,128)S(1)}, s32[1,2]{0,1:T(2,128)S(1)}, u32[]{:S(2)}, u32[]{:S(2)}) collective-permute-start(s32[1,2]{0,1:T(2,128)S(1)} %copy.23), channel_id=1, source_target_pairs={{0,1},{1,2},{2,3},{3,4},{4,5},{5,6},{6,7},{8,9},{9,10},{10,11},{11... | collective-permute-start | bytes 32 | tf_op jit(solution)/shard_map/ppermute | solution.py:16
  9.2 10.7 %collective-permute-start.40 = (s32[1,1]{1,0:T(1,128)}, s32[1,1]{1,0:T(1,128)}, u32[]{:S(2)}, u32[]{:S(2)}) collective-permute-start(s32[1,1]{1,0:T(1,128)} %bitcast.42), channel_id=1, source_target_pairs={{0,16},{16,0},{1,17},{17,1},{2,18},{18,2},{3,19},{19,3},{4,20},{20... | collective-permute-start | bytes 20 | tf_op jit(solution)/shard_map/ppermute | solution.py:24
  16.0 3.8 %copy-start.12 = (f32[8]{0:T(128)S(1)}, f32[8]{0:T(128)}, u32[]{:S(2)}) copy-start(f32[8]{0:T(128)} %param.14) | copy-start | bytes 100
  16.0 3.8 %copy-start.13 = (f32[8]{0:T(128)S(1)}, f32[8]{0:T(128)}, u32[]{:S(2)}) copy-start(f32[8]{0:T(128)} %param.13) | copy-start | bytes 100
  16.0 3.8 %copy-start.11 = (f32[3,8]{1,0:T(4,128)S(1)}, f32[3,8]{1,0:T(4,128)}, u32[]{:S(2)}) copy-start(f32[3,8]{1,0:T(4,128)} %param.15) | copy-start | bytes 292
  16.0 3.8 %copy-start.14 = (f32[8]{0:T(128)S(1)}, f32[8]{0:T(128)}, u32[]{:S(2)}) copy-start(f32[8]{0:T(128)} %param.12) | copy-start | bytes 100
  20.5 24.0 %copy-start.4 = (bf16[480,1024]{1,0:T(8,128)(2,1)}, bf16[480,1024]{1,0:T(8,128)(2,1)S(1)}, u32[]{:S(2)}) copy-start(bf16[480,1024]{1,0:T(8,128)(2,1)S(1)} %get-tuple-element.50) | copy-start | bytes 2949124 | tf_op jit(solution)/shard_map/cond
  23.4 26.3 %copy-start.9 = (bf16[1024,256]{1,0:T(8,128)(2,1)}, bf16[1024,256]{1,0:T(8,128)(2,1)S(1)}, u32[]{:S(2)}) copy-start(bf16[1024,256]{1,0:T(8,128)(2,1)S(1)} %get-tuple-element.103) | copy-start | bytes 1572868 | tf_op jit(solution)/shard_map/cond
  24.7 29.3 %collective-permute-start.22 = (bf16[320,512]{1,0:T(8,128)(2,1)}, bf16[320,512]{1,0:T(8,128)(2,1)S(1)}, u32[]{:S(2)}, u32[]{:S(2)}) collective-permute-start(bf16[320,512]{1,0:T(8,128)(2,1)} %fusion.5), channel_id=1, source_target_pairs={{2,0},{3,1},{4,2},{5,3},{6,4},{7,5},{10,8},{11,9},{12,10},{13,11},... | collective-permute-start | bytes 983048 | tf_op jit(solution)/shard_map/cond/branch_0_fun/ppermute | solution.py:16
  28.2 36.8 %collective-permute-start.21 = (bf16[480,512]{1,0:T(8,128)(2,1)}, bf16[480,512]{1,0:T(8,128)(2,1)S(1)}, u32[]{:S(2)}, u32[]{:S(2)}) collective-permute-start(bf16[480,512]{1,0:T(8,128)(2,1)} %fusion), channel_id=1, source_target_pairs={{1,0},{2,1},{3,2},{4,3},{5,4},{6,5},{7,6},{9,8},{10,9},{11,10},{12... | collective-permute-start | bytes 1474568 | tf_op jit(solution)/shard_map/cond/branch_0_fun/ppermute | solution.py:16
  32.5 23.7 %collective-permute-start.20 = (bf16[320,512]{1,0:T(8,128)(2,1)}, bf16[320,512]{1,0:T(8,128)(2,1)S(1)}, u32[]{:S(2)}, u32[]{:S(2)}) collective-permute-start(bf16[320,512]{1,0:T(8,128)(2,1)} %fusion.4), channel_id=1, source_target_pairs={{0,1},{1,2},{2,3},{3,4},{4,5},{5,6},{6,7},{8,9},{9,10},{10,11},{11... | collective-permute-start | bytes 983048 | tf_op jit(solution)/shard_map/cond/branch_0_fun/ppermute | solution.py:16
  36.2 50.6 %collective-permute-start.26 = (bf16[480,512]{1,0:T(8,128)(2,1)}, bf16[480,512]{1,0:T(8,128)(2,1)S(1)}, u32[]{:S(2)}, u32[]{:S(2)}) collective-permute-start(bf16[480,512]{1,0:T(8,128)(2,1)} %fusion.1), channel_id=1, source_target_pairs={{1,0},{2,1},{3,2},{4,3},{5,4},{6,5},{7,6},{9,8},{10,9},{11,10},{12... | collective-permute-start | bytes 1474568 | tf_op jit(solution)/shard_map/cond/branch_0_fun/ppermute | solution.py:16
  41.3 41.0 %collective-permute-start.25 = (bf16[320,512]{1,0:T(8,128)(2,1)}, bf16[320,512]{1,0:T(8,128)(2,1)S(1)}, u32[]{:S(2)}, u32[]{:S(2)}) collective-permute-start(bf16[320,512]{1,0:T(8,128)(2,1)} %fusion.6), channel_id=1, source_target_pairs={{0,1},{1,2},{2,3},{3,4},{4,5},{5,6},{6,7},{8,9},{9,10},{10,11},{11... | collective-permute-start | bytes 983048 | tf_op jit(solution)/shard_map/cond/branch_0_fun/ppermute | solution.py:16
  51.0 3.0 %copy-start.19 = (bf16[320,512]{1,0:T(8,128)(2,1)S(1)}, bf16[320,512]{1,0:T(8,128)(2,1)}, u32[]{:S(2)}) copy-start(bf16[320,512]{1,0:T(8,128)(2,1)} %fusion.7) | copy-start | bytes 983044 | tf_op jit(solution)/shard_map/cond
  51.0 16.0 %copy-start = (bf16[1024,2048]{1,0:T(8,128)(2,1)S(1)}, bf16[1024,2048]{1,0:T(8,128)(2,1)}, u32[]{:S(2)}) copy-start(bf16[1024,2048]{1,0:T(8,128)(2,1)} %get-tuple-element.48.refs_8_) | copy-start | bytes 12582916 | tf_op jit(solution)/shard_map/cond
  51.0 16.0 %copy-start.5 = (bf16[1024,320]{1,0:T(8,128)(2,1)S(1)}, bf16[1024,320]{1,0:T(8,128)(2,1)}, u32[]{:S(2)}) copy-start(bf16[1024,320]{1,0:T(8,128)(2,1)} %get-tuple-element.45.refs_5_) | copy-start | bytes 1966084 | tf_op jit(solution)/shard_map/cond
  53.9 30.8 %collective-permute-start.27 = (bf16[320,512]{1,0:T(8,128)(2,1)S(1)}, bf16[320,512]{1,0:T(8,128)(2,1)S(1)}, u32[]{:S(2)}, u32[]{:S(2)}) collective-permute-start(bf16[320,512]{1,0:T(8,128)(2,1)S(1)} %copy-done.19), channel_id=1, source_target_pairs={{2,0},{3,1},{4,2},{5,3},{6,4},{7,5},{10,8},{11,9},{12,10},{13,11},... | collective-permute-start | bytes 983048 | tf_op jit(solution)/shard_map/cond/branch_0_fun/ppermute | solution.py:16
  56.1 68.7 %collective-permute-start.31 = (bf16[480,512]{1,0:T(8,128)(2,1)}, bf16[480,512]{1,0:T(8,128)(2,1)S(1)}, u32[]{:S(2)}, u32[]{:S(2)}) collective-permute-start(bf16[480,512]{1,0:T(8,128)(2,1)} %fusion.2), channel_id=1, source_target_pairs={{1,0},{2,1},{3,2},{4,3},{5,4},{6,5},{7,6},{9,8},{10,9},{11,10},{12... | collective-permute-start | bytes 1474568 | tf_op jit(solution)/shard_map/cond/branch_0_fun/ppermute | solution.py:16
  65.0 39.5 %collective-permute-start.30 = (bf16[320,512]{1,0:T(8,128)(2,1)}, bf16[320,512]{1,0:T(8,128)(2,1)S(1)}, u32[]{:S(2)}, u32[]{:S(2)}) collective-permute-start(bf16[320,512]{1,0:T(8,128)(2,1)} %fusion.8), channel_id=1, source_target_pairs={{0,1},{1,2},{2,3},{3,4},{4,5},{5,6},{6,7},{8,9},{9,10},{10,11},{11... | collective-permute-start | bytes 983048 | tf_op jit(solution)/shard_map/cond/branch_0_fun/ppermute | solution.py:16
  66.9 15.5 %copy-start.18 = (bf16[320,512]{1,0:T(8,128)(2,1)S(1)}, bf16[320,512]{1,0:T(8,128)(2,1)}, u32[]{:S(2)}) copy-start(bf16[320,512]{1,0:T(8,128)(2,1)} %fusion.9) | copy-start | bytes 983044 | tf_op jit(solution)/shard_map/cond
  66.9 17.8 %copy-start.17 = (bf16[320,512]{1,0:T(8,128)(2,1)S(1)}, bf16[320,512]{1,0:T(8,128)(2,1)}, u32[]{:S(2)}) copy-start(bf16[320,512]{1,0:T(8,128)(2,1)} %fusion.11) | copy-start | bytes 983044 | tf_op jit(solution)/shard_map/cond
  67.0 24.1 %copy-start.2 = (bf16[1024,1024]{1,0:T(8,128)(2,1)S(1)}, bf16[1024,1024]{1,0:T(8,128)(2,1)}, u32[]{:S(2)}) copy-start(bf16[1024,1024]{1,0:T(8,128)(2,1)} %get-tuple-element.43.refs_3_) | copy-start | bytes 6291460 | tf_op jit(solution)/shard_map/cond
  67.0 24.1 %copy-start.3 = (bf16[1024,1024]{1,0:T(8,128)(2,1)S(1)}, bf16[1024,1024]{1,0:T(8,128)(2,1)}, u32[]{:S(2)}) copy-start(bf16[1024,1024]{1,0:T(8,128)(2,1)} %get-tuple-element.44.refs_4_) | copy-start | bytes 6291460 | tf_op jit(solution)/shard_map/cond
  67.0 24.1 %copy-start.6 = (bf16[1024,320]{1,0:T(8,128)(2,1)S(1)}, bf16[1024,320]{1,0:T(8,128)(2,1)}, u32[]{:S(2)}) copy-start(bf16[1024,320]{1,0:T(8,128)(2,1)} %get-tuple-element.47.refs_7_) | copy-start | bytes 1966084 | tf_op jit(solution)/shard_map/cond
  82.4 22.2 %copy-start.16 = (bf16[320,512]{1,0:T(8,128)(2,1)S(1)}, bf16[320,512]{1,0:T(8,128)(2,1)}, u32[]{:S(2)}) copy-start(bf16[320,512]{1,0:T(8,128)(2,1)} %fusion.10) | copy-start | bytes 983044 | tf_op jit(solution)/shard_map/cond
  82.4 39.6 %collective-permute-start.32 = (bf16[320,512]{1,0:T(8,128)(2,1)S(1)}, bf16[320,512]{1,0:T(8,128)(2,1)S(1)}, u32[]{:S(2)}, u32[]{:S(2)}) collective-permute-start(bf16[320,512]{1,0:T(8,128)(2,1)S(1)} %copy-done.18), channel_id=1, source_target_pairs={{2,0},{3,1},{4,2},{5,3},{6,4},{7,5},{10,8},{11,9},{12,10},{13,11},... | collective-permute-start | bytes 983048 | tf_op jit(solution)/shard_map/cond/branch_0_fun/ppermute | solution.py:16
  84.8 53.6 %collective-permute-start.37 = (bf16[320,512]{1,0:T(8,128)(2,1)S(1)}, bf16[320,512]{1,0:T(8,128)(2,1)S(1)}, u32[]{:S(2)}, u32[]{:S(2)}) collective-permute-start(bf16[320,512]{1,0:T(8,128)(2,1)S(1)} %copy-done.17), channel_id=1, source_target_pairs={{2,0},{3,1},{4,2},{5,3},{6,4},{7,5},{10,8},{11,9},{12,10},{13,11},... | collective-permute-start | bytes 983048 | tf_op jit(solution)/shard_map/cond/branch_0_fun/ppermute | solution.py:16
  86.9 52.0 %collective-permute-start.36 = (bf16[480,512]{1,0:T(8,128)(2,1)}, bf16[480,512]{1,0:T(8,128)(2,1)S(1)}, u32[]{:S(2)}, u32[]{:S(2)}) collective-permute-start(bf16[480,512]{1,0:T(8,128)(2,1)} %fusion.3), channel_id=1, source_target_pairs={{1,0},{2,1},{3,2},{4,3},{5,4},{6,5},{7,6},{9,8},{10,9},{11,10},{12... | collective-permute-start | bytes 1474568 | tf_op jit(solution)/shard_map/cond/branch_0_fun/ppermute | solution.py:16
  104.6 34.3 %collective-permute-start.35 = (bf16[320,512]{1,0:T(8,128)(2,1)S(1)}, bf16[320,512]{1,0:T(8,128)(2,1)S(1)}, u32[]{:S(2)}, u32[]{:S(2)}) collective-permute-start(bf16[320,512]{1,0:T(8,128)(2,1)S(1)} %copy-done.16), channel_id=1, source_target_pairs={{0,1},{1,2},{2,3},{3,4},{4,5},{5,6},{6,7},{8,9},{9,10},{10,11},{11... | collective-permute-start | bytes 983048 | tf_op jit(solution)/shard_map/cond/branch_0_fun/ppermute | solution.py:16
  122.0 30.4 %collective-permute-start.23 = (f32[2,4,16,256]{3,2,1,0:T(8,128)S(1)}, f32[2,4,16,256]{3,2,1,0:T(8,128)S(1)}, u32[]{:S(2)}, u32[]{:S(2)}) collective-permute-start(f32[2,4,16,256]{3,2,1,0:T(8,128)S(1)} %constant_dynamic-slice_fusion.3), channel_id=1, source_target_pairs={{0,8},{8,0},{1,9},{9,1},{2,10},{10,2},{3,11},{11,3},{4,12},{12,4},... | collective-permute-start | bytes 393224 | tf_op jit(solution)/shard_map/cond/branch_0_fun/ppermute | solution.py:193
  124.8 27.6 %collective-permute-start.28 = (f32[2,4,16,256]{3,2,1,0:T(8,128)S(1)}, f32[2,4,16,256]{3,2,1,0:T(8,128)S(1)}, u32[]{:S(2)}, u32[]{:S(2)}) collective-permute-start(f32[2,4,16,256]{3,2,1,0:T(8,128)S(1)} %constant_dynamic-slice_fusion.2), channel_id=1, source_target_pairs={{0,8},{8,0},{1,9},{9,1},{2,10},{10,2},{3,11},{11,3},{4,12},{12,4},... | collective-permute-start | bytes 393224 | tf_op jit(solution)/shard_map/cond/branch_0_fun/ppermute | solution.py:193
  138.4 14.1 %collective-permute-start.33 = (f32[2,4,16,256]{3,2,1,0:T(8,128)S(1)}, f32[2,4,16,256]{3,2,1,0:T(8,128)S(1)}, u32[]{:S(2)}, u32[]{:S(2)}) collective-permute-start(f32[2,4,16,256]{3,2,1,0:T(8,128)S(1)} %constant_dynamic-slice_fusion.1), channel_id=1, source_target_pairs={{0,8},{8,0},{1,9},{9,1},{2,10},{10,2},{3,11},{11,3},{4,12},{12,4},... | collective-permute-start | bytes 393224 | tf_op jit(solution)/shard_map/cond/branch_0_fun/ppermute | solution.py:193
  152.3 1.4 collective-permute-start.38
  154.1 28.0 %collective-permute-start.24 = (f32[4,16,256]{2,1,0:T(8,128)S(1)}, f32[4,16,256]{2,1,0:T(8,128)S(1)}, u32[]{:S(2)}, u32[]{:S(2)}) collective-permute-start(f32[4,16,256]{2,1,0:T(8,128)S(1)} %fusion.35), channel_id=1, source_target_pairs={{1,0},{2,1},{3,2},{4,3},{5,4},{6,5},{7,6},{9,8},{10,9},{11,10},{12... | collective-permute-start | bytes 196616 | tf_op jit(solution)/shard_map/cond/branch_0_fun/ppermute | solution.py:16
  156.1 27.5 %collective-permute-start.29 = (f32[4,16,256]{2,1,0:T(8,128)S(1)}, f32[4,16,256]{2,1,0:T(8,128)S(1)}, u32[]{:S(2)}, u32[]{:S(2)}) collective-permute-start(f32[4,16,256]{2,1,0:T(8,128)S(1)} %fusion.34), channel_id=1, source_target_pairs={{1,0},{2,1},{3,2},{4,3},{5,4},{6,5},{7,6},{9,8},{10,9},{11,10},{12... | collective-permute-start | bytes 196616 | tf_op jit(solution)/shard_map/cond/branch_0_fun/ppermute | solution.py:16
  158.1 27.0 %collective-permute-start.34 = (f32[4,16,256]{2,1,0:T(8,128)S(1)}, f32[4,16,256]{2,1,0:T(8,128)S(1)}, u32[]{:S(2)}, u32[]{:S(2)}) collective-permute-start(f32[4,16,256]{2,1,0:T(8,128)S(1)} %fusion.33), channel_id=1, source_target_pairs={{1,0},{2,1},{3,2},{4,3},{5,4},{6,5},{7,6},{9,8},{10,9},{11,10},{12... | collective-permute-start | bytes 196616 | tf_op jit(solution)/shard_map/cond/branch_0_fun/ppermute | solution.py:16
  160.1 26.4 %collective-permute-start.39 = (f32[4,16,256]{2,1,0:T(8,128)S(1)}, f32[4,16,256]{2,1,0:T(8,128)S(1)}, u32[]{:S(2)}, u32[]{:S(2)}) collective-permute-start(f32[4,16,256]{2,1,0:T(8,128)S(1)} %fusion.32), channel_id=1, source_target_pairs={{1,0},{2,1},{3,2},{4,3},{5,4},{6,5},{7,6},{9,8},{10,9},{11,10},{12... | collective-permute-start | bytes 196616 | tf_op jit(solution)/shard_map/cond/branch_0_fun/ppermute | solution.py:16
  187.0 0.7 copy-start.10

commit v3 on v2

--- a/solution.py
+++ b/solution.py
@@ -6,8 +6,8 @@
 from jax.experimental.pallas import tpu as pltpu
 from jax.sharding import PartitionSpec as P
 
-CHUNKS = 4
-LANES = 128
+CHUNKS = 2
+BLOCK = 256
 
 
 def along_lat(block, distance):
@@ -92,34 +92,32 @@
 
     def cast(band, limit):
         forward = front_ref[0, band] == 0
-        for part in range(out_ref.shape[3] // LANES):
-            lanes = slice(part * LANES, (part + 1) * LANES)
-            zero = jnp.zeros((rows, LANES), jnp.float32)
-            empty = None if limit is None else classify(zero)
-
-            def advance(i, carry):
-                depth, clear, red, green, blue = carry
-                z = jnp.where(forward, i, slices - 1 - i)
-
-                def filled():
-                    return classify(cells[pl.ds(pl.multiple_of(z * rows, rows), rows), lanes])
-
-                if limit is None:
-                    sums = filled()
-                else:
-                    sums = lax.cond(shift_ref[0, z] >= limit, lambda: empty, filled)
-                depth = depth + sums[0]
-                after = jnp.exp2(-depth)
-                weight = clear - after
-                return (depth, after, red + weight * sums[1], green + weight * sums[2], blue + weight * sums[3])
-
-            depth, _, red, green, blue = lax.fori_loop(
-                0, slices, advance, (zero, zero + 1.0, zero, zero, zero), unroll=2 if limit is None else 1
-            )
-            out_ref[band, 0, :, lanes] = red
-            out_ref[band, 1, :, lanes] = green
-            out_ref[band, 2, :, lanes] = blue
-            out_ref[band, 3, :, lanes] = depth
+        zero = jnp.zeros((rows, out_ref.shape[3]), jnp.float32)
+        empty = None if limit is None else classify(zero)
+
+        def advance(i, carry):
+            depth, clear, red, green, blue = carry
+            z = jnp.where(forward, i, slices - 1 - i)
+
+            def filled():
+                return classify(cells[pl.ds(pl.multiple_of(z * rows, rows), rows), :])
+
+            if limit is None:
+                sums = filled()
+            else:
+                sums = lax.cond(shift_ref[0, z] >= limit, lambda: empty, filled)
+            depth = depth + sums[0]
+            after = jnp.exp2(-depth)
+            weight = clear - after
+            return (depth, after, red + weight * sums[1], green + weight * sums[2], blue + weight * sums[3])
+
+        depth, _, red, green, blue = lax.fori_loop(
+            0, slices, advance, (zero, zero + 1.0, zero, zero, zero), unroll=2 if limit is None else 1
+        )
+        out_ref[band, 0] = red
+        out_ref[band, 1] = green
+        out_ref[band, 2] = blue
+        out_ref[band, 3] = depth
 
     fill([(own_m, own), (up_m, up), (one_m, one), (two_m, two)])
 
@@ -139,8 +137,10 @@
     slices = shift.shape[1]
     total, cols = field.shape
     rows = total // slices
-    block = cols // slabs // CHUNKS
+    width = cols // slabs // CHUNKS
+    block = min(BLOCK, width)
     stride = cols // slabs // block
+    steps = width // block
 
     def whole(m):
         return pl.BlockSpec(m.shape, lambda c: (0, 0))
@@ -149,15 +149,15 @@
         return pl.BlockSpec((a.shape[0], block), lambda c: (0, c))
 
     smem = pl.BlockSpec(memory_space=pltpu.SMEM)
-    cells = total * block * slabs
+    cells = total * width * slabs
     last = lax.axis_size("lat") - 1
     return pl.pallas_call(
         lambda *refs: render_kernel(slices, rows, last, *refs),
-        out_shape=jax.ShapeDtypeStruct((2, 4, rows, block * slabs), jnp.float32),
-        grid=(slabs,),
+        out_shape=jax.ShapeDtypeStruct((2, 4, rows, width * slabs), jnp.float32),
+        grid=(slabs * steps,),
         in_specs=[smem] * 3
         + [whole(m) for m in unpacks]
-        + [pl.BlockSpec((total, block), lambda c: (0, c * stride + chunk))]
+        + [pl.BlockSpec((total, block), lambda c: (0, c // steps * stride + chunk * steps + c % steps))]
         + [columns(a) for a in (up, one, two)],
         out_specs=pl.BlockSpec((2, 4, rows, block), lambda c: (0, 0, 0, c)),
         scratch_shapes=[pltpu.VMEM((total, block), jnp.float32)],

time: 189 us -> 167 us (0.88)
  the two profiles are of different devices: /device:TPU:27 before, /device:TPU:24 now
where the time goes in v3:
time: 167 us; the launch traced here: 169 us
  Pallas kernels  53.2 us (32%)
  waiting for transfers between devices  47.4 us (28%)
  starting transfers between devices  34 us (20%)
  matrix products  12.8 us (8%)
  other arithmetic  10.2 us (6%)
  local copies, waits for them, and re-layouts  6.26 us (4%)
  between operations  4.6 us (3%)
    pallas_call x2, Pallas kernels, render(): pl.pallas_call(lambda *refs: render_kernel(slices, rows, last, *refs), ou...  53.2 us
    ppermute x9, waiting for transfers between devices, along_lat(): return lax.ppermute(block, 'lat', route)  45.9 us
    ppermute x9, starting transfers between devices, along_lat(): return lax.ppermute(block, 'lat', route)  31 us
    dot_general x6, matrix products, pick(): jnp.dot(matrix, rows, preferred_element_type=jnp.float32)  12.8 us
    convert_element_type x5, other arithmetic, unpack(): (there == jnp.arange(count, dtype=jnp.int32)[None, :]).astype(jnp.bfloat16)  6.92 us
  transfers between devices with their start and end apart: 12, of which 6 were waited for; matrix products, arithmetic and copies ran while one was open for 13% of the time, Pallas kernels for 31%

profile of v3, /device:TPU:24, one launch (start us, length us, event | category | flops | bytes accessed | tf_op | source)
XLA Modules:
  0.0 168.9 jit_solution(4191787617948218364)
XLA Ops:
  0.0 0.7 copy.23
  0.7 3.4 %collective-permute-start.21 = (s32[1,2]{0,1:T(2,128)S(1)}, s32[1,2]{0,1:T(2,128)S(1)}, u32[]{:S(2)}, u32[]{:S(2)}) collective-permute-start(s32[1,2]{0,1:T(2,128)S(1)} %copy.23), channel_id=1, source_target_pairs={{0,1},{1,2},{2,3},{3,4},{4,5},{5,6},{6,7},{8,9},{9,10},{10,11},{11... | collective-permute-start | bytes 32 | tf_op jit(solution)/shard_map/ppermute | solution.py:16
  4.2 0.7 add_select_fusion.6
  4.8 0.8 convert_reduce_fusion
  9.4 2.9 %collective-permute-start.20 = (s32[1,1]{1,0:T(1,128)}, s32[1,1]{1,0:T(1,128)}, u32[]{:S(2)}, u32[]{:S(2)}) collective-permute-start(s32[1,1]{1,0:T(1,128)} %bitcast.24), channel_id=1, source_target_pairs={{0,16},{16,0},{1,17},{17,1},{2,18},{18,2},{3,19},{19,3},{4,20},{20... | collective-permute-start | bytes 20 | tf_op jit(solution)/shard_map/ppermute | solution.py:24
  12.3 0.7 dynamic_slice.27
  13.1 0.1 select_reduce_fusion.21
  13.2 0.1 select_reduce_fusion.19
  13.3 0.2 select_reduce_fusion.16
  13.5 0.2 select_reduce_fusion.11
  13.7 0.1 copy.29
  13.9 1.8 %fusion.111 = bf16[1024,1024]{1,0:T(8,128)(2,1)} fusion(s32[1024]{0:T(1024)S(1)} %eq.452), kind=kLoop, calls=%fused_computation.212 | loop fusion | flops 2097152 | bytes 2101248 | tf_op jit(solution)/shard_map/convert_element_type | solution.py:58
  15.8 1.7 %fusion.112 = bf16[1024,1024]{1,0:T(8,128)(2,1)} fusion(s32[1024]{0:T(1024)S(1)} %eq.456), kind=kLoop, calls=%fused_computation.213 | loop fusion | flops 2097152 | bytes 2101248 | tf_op jit(solution)/shard_map/convert_element_type | solution.py:58
  17.5 0.1 copy.32
  17.7 1.2 fusion.113
  19.1 1.1 fusion.115
  20.4 1.1 fusion.116
  21.5 0.1 copy.28
  22.2 0.3 fusion.114
  22.5 0.1 fusion.117
  22.7 0.1 fusion.118
  23.6 144.6 %conditional.1 = (f32[4,16,1024]{2,1,0:T(8,128)S(1)}) conditional(s32[]{:T(128)} %bitcast.25, (s32[2,2]{0,1:T(2,128)S(1)}, s32[64]{0:T(128)S(1)}, bf16[1024,2048]{1,0:T(8,128)(2,1)}, bf16[320,1024]{1,0:T(8,128)(2,1)S(1)}, bf16[480,1024]{1,0:T(8,128)(2,1)S(1)}, /*index=5*/bf16[320,1024]{1,0:T(8,128)(2,1)S(1)}, f32[6,8]{1,0:T(8,128)S(1)}, ...), branch_computations={%region_20.21_spmd, %region_21.36_spmd} | conditional | flops 63266123776 | bytes 142984384 | solution.py:226
  23.6 2.5 %fusion.144 = (bf16[1024,512]{1,0:T(8,128)(2,1)S(1)}, bf16[1024,512]{1,0:T(8,128)(2,1)S(1)}, bf16[1024,512]{1,0:T(8,128)(2,1)S(1)}, bf16[1024,512]{1,0:T(8,128)(2,1)S(1)}) fusion(bf16[1024,2048]{1,0:T(8,128)(2,1)} %get-tuple-element.48.refs_8_), kind=kLoop, calls=%fused_computation.312 | loop fusion | bytes 8388608 | tf_op jit(solution)/shard_map/cond/branch_0_fun/slice | solution.py:184
  26.1 2.2 %fusion = bf16[480,1024]{1,0:T(8,128)(2,1)} fusion(bf16[480,1024]{1,0:T(8,128)(2,1)S(1)} %get-tuple-element.50, bf16[1024,512]{1,0:T(8,128)(2,1)S(1)} %get-tuple-element.104, bf16[1024,512]{1,0:T(8,128)(2,1)S(1)} %get-tuple-element.101), kind=kOutput, calls=%fused_computation.4 | convolution fusion | flops 1011318784 | bytes 4063232 | tf_op jit(solution)/shard_map/cond/branch_0_fun/dot_general | solution.py:171
  28.3 3.3 %collective-permute-start.11 = (bf16[480,1024]{1,0:T(8,128)(2,1)}, bf16[480,1024]{1,0:T(8,128)(2,1)S(1)}, u32[]{:S(2)}, u32[]{:S(2)}) collective-permute-start(bf16[480,1024]{1,0:T(8,128)(2,1)} %fusion), channel_id=1, source_target_pairs={{1,0},{2,1},{3,2},{4,3},{5,4},{6,5},{7,6},{9,8},{10,9},{11,10},{12... | collective-permute-start | bytes 2949128 | tf_op jit(solution)/shard_map/cond/branch_0_fun/ppermute | solution.py:16
  31.6 1.7 %fusion.2 = bf16[320,1024]{1,0:T(8,128)(2,1)} fusion(bf16[320,1024]{1,0:T(8,128)(2,1)S(1)} %get-tuple-element.49, bf16[1024,512]{1,0:T(8,128)(2,1)S(1)} %get-tuple-element.104, bf16[1024,512]{1,0:T(8,128)(2,1)S(1)} %get-tuple-element.101), kind=kOutput, calls=%fused_computation.10 | convolution fusion | flops 675610624 | bytes 3407872 | tf_op jit(solution)/shard_map/cond/branch_0_fun/dot_general | solution.py:171
  33.3 2.6 %collective-permute-start.10 = (bf16[320,1024]{1,0:T(8,128)(2,1)}, bf16[320,1024]{1,0:T(8,128)(2,1)}, u32[]{:S(2)}, u32[]{:S(2)}) collective-permute-start(bf16[320,1024]{1,0:T(8,128)(2,1)} %fusion.2), channel_id=1, source_target_pairs={{0,1},{1,2},{2,3},{3,4},{4,5},{5,6},{6,7},{8,9},{9,10},{10,11},{11... | collective-permute-start | bytes 1966088 | tf_op jit(solution)/shard_map/cond/branch_0_fun/ppermute | solution.py:16
  35.8 1.7 fusion.3
  37.5 3.1 %collective-permute-start.12 = (bf16[320,1024]{1,0:T(8,128)(2,1)}, bf16[320,1024]{1,0:T(8,128)(2,1)}, u32[]{:S(2)}, u32[]{:S(2)}) collective-permute-start(bf16[320,1024]{1,0:T(8,128)(2,1)} %fusion.3), channel_id=1, source_target_pairs={{2,0},{3,1},{4,2},{5,3},{6,4},{7,5},{10,8},{11,9},{12,10},{13,11},... | collective-permute-start | bytes 1966088 | tf_op jit(solution)/shard_map/cond/branch_0_fun/ppermute | solution.py:16
  40.6 1.7 %fusion.5 = bf16[320,1024]{1,0:T(8,128)(2,1)} fusion(bf16[320,1024]{1,0:T(8,128)(2,1)S(1)} %get-tuple-element.51, bf16[1024,512]{1,0:T(8,128)(2,1)S(1)} %get-tuple-element.102, bf16[1024,512]{1,0:T(8,128)(2,1)S(1)} %get-tuple-element.103), kind=kOutput, calls=%fused_computation.13 | convolution fusion | flops 675610624 | bytes 3407872 | tf_op jit(solution)/shard_map/cond/branch_0_fun/dot_general | solution.py:171
  42.4 1.5 collective-permute-start.17
  44.0 2.1 %fusion.1 = bf16[480,1024]{1,0:T(8,128)(2,1)} fusion(bf16[480,1024]{1,0:T(8,128)(2,1)S(1)} %get-tuple-element.50, bf16[1024,512]{1,0:T(8,128)(2,1)S(1)} %get-tuple-element.102, bf16[1024,512]{1,0:T(8,128)(2,1)S(1)} %get-tuple-element.103), kind=kOutput, calls=%fused_computation.5 | convolution fusion | flops 1011318784 | bytes 4063232 | tf_op jit(solution)/shard_map/cond/branch_0_fun/dot_general | solution.py:171
  46.1 4.2 %collective-permute-start.16 = (bf16[480,1024]{1,0:T(8,128)(2,1)}, bf16[480,1024]{1,0:T(8,128)(2,1)S(1)}, u32[]{:S(2)}, u32[]{:S(2)}) collective-permute-start(bf16[480,1024]{1,0:T(8,128)(2,1)} %fusion.1), channel_id=1, source_target_pairs={{1,0},{2,1},{3,2},{4,3},{5,4},{6,5},{7,6},{9,8},{10,9},{11,10},{12... | collective-permute-start | bytes 2949128 | tf_op jit(solution)/shard_map/cond/branch_0_fun/ppermute | solution.py:16
  50.3 3.4 %fusion.4 = bf16[320,1024]{1,0:T(8,128)(2,1)} fusion(bf16[320,1024]{1,0:T(8,128)(2,1)S(1)} %get-tuple-element.49, bf16[1024,512]{1,0:T(8,128)(2,1)} %copy-done.5, bf16[1024,512]{1,0:T(8,128)(2,1)} %copy-done.6), kind=kOutput, calls=%fused_computation.12 | convolution fusion | flops 675610624 | bytes 3407872 | tf_op jit(solution)/shard_map/cond/branch_0_fun/dot_general | solution.py:171
  53.7 1.9 %collective-permute-start.15 = (bf16[320,1024]{1,0:T(8,128)(2,1)}, bf16[320,1024]{1,0:T(8,128)(2,1)S(1)}, u32[]{:S(2)}, u32[]{:S(2)}) collective-permute-start(bf16[320,1024]{1,0:T(8,128)(2,1)} %fusion.4), channel_id=1, source_target_pairs={{0,1},{1,2},{2,3},{3,4},{4,5},{5,6},{6,7},{8,9},{9,10},{10,11},{11... | collective-permute-start | bytes 1966088 | tf_op jit(solution)/shard_map/cond/branch_0_fun/ppermute | solution.py:16
  55.6 12.5 %collective-permute-done.12.refs_11_ = bf16[320,1024]{1,0:T(8,128)(2,1)} collective-permute-done((bf16[320,1024]{1,0:T(8,128)(2,1)}, bf16[320,1024]{1,0:T(8,128)(2,1)}, u32[]{:S(2)}, u32[]{:S(2)}) %collective-permute-start.12) | collective-permute-done | bytes 655392 | tf_op jit(solution)/shard_map/cond/branch_0_fun/ppermute | solution.py:16
  68.2 0.9 collective-permute-done.11.refs_10_
  69.1 27.6 %render.4 = f32[2,4,16,1024]{3,2,1,0:T(8,128)S(1)} custom-call(s32[1,2]{1,0:T(1,128)S(1)} %slice_bitcast_fusion.refs_0_, s32[1,64]{1,0:T(1,128)S(1)} %bitcast.70, f32[6,8]{1,0:T(8,128)S(1)} %get-tuple-element.42.refs_2_, bf16[1024,1024]{1,0:T(8,128)(2,1)S(1)} %copy-done.2, bf16[1024,1024]{1,0:T(8,128)(2,1)} %get-tuple-element.44.refs_4_, ...), custom_call_target="tpu_custom_call" | custom-call | flops 25165824000 | bytes 6291456 | tf_op jit(solution)/shard_map/cond/branch_0_fun/render/pallas_call | solution.py:154
  96.8 5.0 %collective-permute-done.16.refs_10_ = bf16[480,1024]{1,0:T(8,128)(2,1)S(1)} collective-permute-done((bf16[480,1024]{1,0:T(8,128)(2,1)}, bf16[480,1024]{1,0:T(8,128)(2,1)S(1)}, u32[]{:S(2)}, u32[]{:S(2)}) %collective-permute-start.16) | collective-permute-done | bytes 983072 | tf_op jit(solution)/shard_map/cond/branch_0_fun/ppermute | solution.py:16
  101.9 25.6 %render.5 = f32[2,4,16,1024]{3,2,1,0:T(8,128)S(1)} custom-call(s32[1,2]{1,0:T(1,128)S(1)} %slice_bitcast_fusion.refs_0_, s32[1,64]{1,0:T(1,128)S(1)} %bitcast.71, f32[6,8]{1,0:T(8,128)S(1)} %get-tuple-element.42.refs_2_, bf16[1024,1024]{1,0:T(8,128)(2,1)S(1)} %copy-done.2, bf16[1024,1024]{1,0:T(8,128)(2,1)S(1)} %copy-done.3, ...), custom_call_target="tpu_custom_call" | custom-call | flops 25165824000 | bytes 6291456 | tf_op jit(solution)/shard_map/cond/branch_0_fun/render/pallas_call | solution.py:154
  127.6 1.5 collective-permute-done.18
  129.1 0.1 dynamic-slice_select_fusion.1
  129.3 0.2 fusion.9
  129.6 9.0 %collective-permute-start.14 = (f32[4,16,512]{2,1,0:T(8,128)S(1)}, f32[4,16,512]{2,1,0:T(8,128)S(1)}, u32[]{:S(2)}, u32[]{:S(2)}) collective-permute-start(f32[4,16,512]{2,1,0:T(8,128)S(1)} %fusion.17), channel_id=1, source_target_pairs={{1,0},{2,1},{3,2},{4,3},{5,4},{6,5},{7,6},{9,8},{10,9},{11,10},{12... | collective-permute-start | bytes 393224 | tf_op jit(solution)/shard_map/cond/branch_0_fun/ppermute | solution.py:16
  138.6 1.9 %collective-permute-start.19 = (f32[4,16,512]{2,1,0:T(8,128)S(1)}, f32[4,16,512]{2,1,0:T(8,128)S(1)}, u32[]{:S(2)}, u32[]{:S(2)}) collective-permute-start(f32[4,16,512]{2,1,0:T(8,128)S(1)} %fusion.16), channel_id=1, source_target_pairs={{1,0},{2,1},{3,2},{4,3},{5,4},{6,5},{7,6},{9,8},{10,9},{11,10},{12... | collective-permute-start | bytes 393224 | tf_op jit(solution)/shard_map/cond/branch_0_fun/ppermute | solution.py:16
  140.6 24.9 %collective-permute-done.14 = f32[4,16,512]{2,1,0:T(8,128)S(1)} collective-permute-done((f32[4,16,512]{2,1,0:T(8,128)S(1)}, f32[4,16,512]{2,1,0:T(8,128)S(1)}, u32[]{:S(2)}, u32[]{:S(2)}) %collective-permute-start.14) | collective-permute-done | bytes 131104 | tf_op jit(solution)/shard_map/cond/branch_0_fun/ppermute | solution.py:16
  165.5 2.5 %collective-permute-done.19 = f32[4,16,512]{2,1,0:T(8,128)S(1)} collective-permute-done((f32[4,16,512]{2,1,0:T(8,128)S(1)}, f32[4,16,512]{2,1,0:T(8,128)S(1)}, u32[]{:S(2)}, u32[]{:S(2)}) %collective-permute-start.19) | collective-permute-done | bytes 131104 | tf_op jit(solution)/shard_map/cond/branch_0_fun/ppermute | solution.py:16
  168.2 0.7 copy-done.9
  (71 shorter events, 1.9 us)
Async XLA Ops:
  0.7 22.8 %collective-permute-start.21 = (s32[1,2]{0,1:T(2,128)S(1)}, s32[1,2]{0,1:T(2,128)S(1)}, u32[]{:S(2)}, u32[]{:S(2)}) collective-permute-start(s32[1,2]{0,1:T(2,128)S(1)} %copy.23), channel_id=1, source_target_pairs={{0,1},{1,2},{2,3},{3,4},{4,5},{5,6},{6,7},{8,9},{9,10},{10,11},{11... | collective-permute-start | bytes 32 | tf_op jit(solution)/shard_map/ppermute | solution.py:16
  9.4 13.5 %collective-permute-start.20 = (s32[1,1]{1,0:T(1,128)}, s32[1,1]{1,0:T(1,128)}, u32[]{:S(2)}, u32[]{:S(2)}) collective-permute-start(s32[1,1]{1,0:T(1,128)} %bitcast.24), channel_id=1, source_target_pairs={{0,16},{16,0},{1,17},{17,1},{2,18},{18,2},{3,19},{19,3},{4,20},{20... | collective-permute-start | bytes 20 | tf_op jit(solution)/shard_map/ppermute | solution.py:24
  19.1 3.8 %copy-start.11 = (f32[8]{0:T(128)S(1)}, f32[8]{0:T(128)}, u32[]{:S(2)}) copy-start(f32[8]{0:T(128)} %param.14) | copy-start | bytes 100
  19.1 3.8 %copy-start.12 = (f32[8]{0:T(128)S(1)}, f32[8]{0:T(128)}, u32[]{:S(2)}) copy-start(f32[8]{0:T(128)} %param.13) | copy-start | bytes 100
  19.1 3.8 %copy-start.10 = (f32[3,8]{1,0:T(4,128)S(1)}, f32[3,8]{1,0:T(4,128)}, u32[]{:S(2)}) copy-start(f32[3,8]{1,0:T(4,128)} %param.15) | copy-start | bytes 292
  19.1 3.8 %copy-start.13 = (f32[8]{0:T(128)S(1)}, f32[8]{0:T(128)}, u32[]{:S(2)}) copy-start(f32[8]{0:T(128)} %param.12) | copy-start | bytes 100
  26.1 17.9 %copy-start.5 = (bf16[1024,512]{1,0:T(8,128)(2,1)}, bf16[1024,512]{1,0:T(8,128)(2,1)S(1)}, u32[]{:S(2)}) copy-start(bf16[1024,512]{1,0:T(8,128)(2,1)S(1)} %get-tuple-element.102) | copy-start | bytes 3145732 | tf_op jit(solution)/shard_map/cond
  26.1 17.9 %copy-start.6 = (bf16[1024,512]{1,0:T(8,128)(2,1)}, bf16[1024,512]{1,0:T(8,128)(2,1)S(1)}, u32[]{:S(2)}) copy-start(bf16[1024,512]{1,0:T(8,128)(2,1)S(1)} %get-tuple-element.103) | copy-start | bytes 3145732 | tf_op jit(solution)/shard_map/cond
  28.3 40.8 %collective-permute-start.11 = (bf16[480,1024]{1,0:T(8,128)(2,1)}, bf16[480,1024]{1,0:T(8,128)(2,1)S(1)}, u32[]{:S(2)}, u32[]{:S(2)}) collective-permute-start(bf16[480,1024]{1,0:T(8,128)(2,1)} %fusion), channel_id=1, source_target_pairs={{1,0},{2,1},{3,2},{4,3},{5,4},{6,5},{7,6},{9,8},{10,9},{11,10},{12... | collective-permute-start | bytes 2949128 | tf_op jit(solution)/shard_map/cond/branch_0_fun/ppermute | solution.py:16
  33.3 20.5 %collective-permute-start.10 = (bf16[320,1024]{1,0:T(8,128)(2,1)}, bf16[320,1024]{1,0:T(8,128)(2,1)}, u32[]{:S(2)}, u32[]{:S(2)}) collective-permute-start(bf16[320,1024]{1,0:T(8,128)(2,1)} %fusion.2), channel_id=1, source_target_pairs={{0,1},{1,2},{2,3},{3,4},{4,5},{5,6},{6,7},{8,9},{9,10},{10,11},{11... | collective-permute-start | bytes 1966088 | tf_op jit(solution)/shard_map/cond/branch_0_fun/ppermute | solution.py:16
  37.5 30.6 %collective-permute-start.12 = (bf16[320,1024]{1,0:T(8,128)(2,1)}, bf16[320,1024]{1,0:T(8,128)(2,1)}, u32[]{:S(2)}, u32[]{:S(2)}) collective-permute-start(bf16[320,1024]{1,0:T(8,128)(2,1)} %fusion.3), channel_id=1, source_target_pairs={{2,0},{3,1},{4,2},{5,3},{6,4},{7,5},{10,8},{11,9},{12,10},{13,11},... | collective-permute-start | bytes 1966088 | tf_op jit(solution)/shard_map/cond/branch_0_fun/ppermute | solution.py:16
  42.4 54.4 %collective-permute-start.17 = (bf16[320,1024]{1,0:T(8,128)(2,1)}, bf16[320,1024]{1,0:T(8,128)(2,1)S(1)}, u32[]{:S(2)}, u32[]{:S(2)}) collective-permute-start(bf16[320,1024]{1,0:T(8,128)(2,1)} %fusion.5), channel_id=1, source_target_pairs={{2,0},{3,1},{4,2},{5,3},{6,4},{7,5},{10,8},{11,9},{12,10},{13,11},... | collective-permute-start | bytes 1966088 | tf_op jit(solution)/shard_map/cond/branch_0_fun/ppermute | solution.py:16
  46.1 55.8 %collective-permute-start.16 = (bf16[480,1024]{1,0:T(8,128)(2,1)}, bf16[480,1024]{1,0:T(8,128)(2,1)S(1)}, u32[]{:S(2)}, u32[]{:S(2)}) collective-permute-start(bf16[480,1024]{1,0:T(8,128)(2,1)} %fusion.1), channel_id=1, source_target_pairs={{1,0},{2,1},{3,2},{4,3},{5,4},{6,5},{7,6},{9,8},{10,9},{11,10},{12... | collective-permute-start | bytes 2949128 | tf_op jit(solution)/shard_map/cond/branch_0_fun/ppermute | solution.py:16
  50.3 18.8 %copy-start = (bf16[1024,2048]{1,0:T(8,128)(2,1)S(1)}, bf16[1024,2048]{1,0:T(8,128)(2,1)}, u32[]{:S(2)}) copy-start(bf16[1024,2048]{1,0:T(8,128)(2,1)} %get-tuple-element.48.refs_8_) | copy-start | bytes 12582916 | tf_op jit(solution)/shard_map/cond
  50.3 18.8 %copy-start.2 = (bf16[1024,1024]{1,0:T(8,128)(2,1)S(1)}, bf16[1024,1024]{1,0:T(8,128)(2,1)}, u32[]{:S(2)}) copy-start(bf16[1024,1024]{1,0:T(8,128)(2,1)} %get-tuple-element.43.refs_3_) | copy-start | bytes 6291460 | tf_op jit(solution)/shard_map/cond
  53.7 43.1 %collective-permute-start.15 = (bf16[320,1024]{1,0:T(8,128)(2,1)}, bf16[320,1024]{1,0:T(8,128)(2,1)S(1)}, u32[]{:S(2)}, u32[]{:S(2)}) collective-permute-start(bf16[320,1024]{1,0:T(8,128)(2,1)} %fusion.4), channel_id=1, source_target_pairs={{0,1},{1,2},{2,3},{3,4},{4,5},{5,6},{6,7},{8,9},{9,10},{10,11},{11... | collective-permute-start | bytes 1966088 | tf_op jit(solution)/shard_map/cond/branch_0_fun/ppermute | solution.py:16
  69.1 32.8 %copy-start.3 = (bf16[1024,1024]{1,0:T(8,128)(2,1)S(1)}, bf16[1024,1024]{1,0:T(8,128)(2,1)}, u32[]{:S(2)}) copy-start(bf16[1024,1024]{1,0:T(8,128)(2,1)} %get-tuple-element.44.refs_4_) | copy-start | bytes 6291460 | tf_op jit(solution)/shard_map/cond
  69.1 32.8 %copy-start.4 = (bf16[1024,480]{1,0:T(8,128)(2,1)S(1)}, bf16[1024,480]{1,0:T(8,128)(2,1)}, u32[]{:S(2)}) copy-start(bf16[1024,480]{1,0:T(8,128)(2,1)} %get-tuple-element.46.refs_6_) | copy-start | bytes 2949124 | tf_op jit(solution)/shard_map/cond
  69.1 32.8 %copy-start.7 = (bf16[1024,320]{1,0:T(8,128)(2,1)S(1)}, bf16[1024,320]{1,0:T(8,128)(2,1)}, u32[]{:S(2)}) copy-start(bf16[1024,320]{1,0:T(8,128)(2,1)} %get-tuple-element.45.refs_5_) | copy-start | bytes 1966084 | tf_op jit(solution)/shard_map/cond
  69.1 32.8 %copy-start.8 = (bf16[1024,320]{1,0:T(8,128)(2,1)S(1)}, bf16[1024,320]{1,0:T(8,128)(2,1)}, u32[]{:S(2)}) copy-start(bf16[1024,320]{1,0:T(8,128)(2,1)} %get-tuple-element.47.refs_7_) | copy-start | bytes 1966084 | tf_op jit(solution)/shard_map/cond
  96.7 30.9 %collective-permute-start.13 = (f32[2,4,16,512]{3,2,1,0:T(8,128)S(1)}, f32[2,4,16,512]{3,2,1,0:T(8,128)S(1)}, u32[]{:S(2)}, u32[]{:S(2)}) collective-permute-start(f32[2,4,16,512]{3,2,1,0:T(8,128)S(1)} %constant_dynamic-slice_fusion.1), channel_id=1, source_target_pairs={{0,8},{8,0},{1,9},{9,1},{2,10},{10,2},{3,11},{11,3},{4,12},{12,4},... | collective-permute-start | bytes 786440 | tf_op jit(solution)/shard_map/cond/branch_0_fun/ppermute | solution.py:193
  127.5 1.6 collective-permute-start.18
  129.6 35.9 %collective-permute-start.14 = (f32[4,16,512]{2,1,0:T(8,128)S(1)}, f32[4,16,512]{2,1,0:T(8,128)S(1)}, u32[]{:S(2)}, u32[]{:S(2)}) collective-permute-start(f32[4,16,512]{2,1,0:T(8,128)S(1)} %fusion.17), channel_id=1, source_target_pairs={{1,0},{2,1},{3,2},{4,3},{5,4},{6,5},{7,6},{9,8},{10,9},{11,10},{12... | collective-permute-start | bytes 393224 | tf_op jit(solution)/shard_map/cond/branch_0_fun/ppermute | solution.py:16
  138.6 29.3 %collective-permute-start.19 = (f32[4,16,512]{2,1,0:T(8,128)S(1)}, f32[4,16,512]{2,1,0:T(8,128)S(1)}, u32[]{:S(2)}, u32[]{:S(2)}) collective-permute-start(f32[4,16,512]{2,1,0:T(8,128)S(1)} %fusion.16), channel_id=1, source_target_pairs={{1,0},{2,1},{3,2},{4,3},{5,4},{6,5},{7,6},{9,8},{10,9},{11,10},{12... | collective-permute-start | bytes 393224 | tf_op jit(solution)/shard_map/cond/branch_0_fun/ppermute | solution.py:16
  168.2 0.7 copy-start.9
